TPU v7x, 256 devices: a whole 4x4x8 slice. The times are simulated.
256 devices in a mesh: shot: 16 (over x, z_lo), tm: 16 (over z_hi, y, core).
Axes of the slice: x: 4, y: 4, z: 8 (z_hi: 2, z_lo: 4; z = z_hi * 4 + z_lo), core: 2. Of those that a mesh axis runs over, the one named last changes fastest.
Arguments:
- noisy_gather: float32 [32, 1024, 128], P('shot', 'tm'), may hold values from -6 to 6
- observed: float32 [32, 1024, 128], P(None, 'tm', 'shot')
- missing: int32 [32, 128], P('shot'), may hold values 0 or 1
- noise_level: float32 [32], P('shot'), may hold values from 0.05 to 0.95
- dilations: int32 [2], replicated, may hold values from 1 to 16, as said below
- lift_weight: float32 [3, 64], replicated, may hold values from -4 to 4
- level_weight: float32 [64], replicated, may hold values from -4 to 4
- norm_gain: float32 [2, 64], replicated, may hold values from 0.1 to 1.9
- conv_weight: bfloat16 [2, 9, 64, 256], replicated, may hold values from -0.25 to 0.25
- out_weight: bfloat16 [2, 256, 64], replicated, may hold values from -0.375 to 0.375
- head_weight: float32 [64], replicated, may hold values from -0.75 to 0.75
Outputs:
- predicted_noise: float32 [32, 1024, 128], P('shot', 'tm')
Inputs may be any that keep to these rules, and one draw needn't show every extreme that they name: `dilations`: each dilation is 1, 2, 4, 8 or 16, and one of them is 16.
All inputs are finite; a program needn't handle non-finite values. No bound on the sum of `missing` on one device may be relied on, other than what follows from the above.
Results may differ from a plain program's by a relative error of at most 0.0039.
Values may be sent and summed in bfloat16 or wider, within the bound.
A program may use at most 128 MiB of HBM per device.

v0:
```python
import jax
import jax.numpy as jnp
from jax import lax
from jax.sharding import PartitionSpec as P

LAYERS = 2
DMAX = 16


def with_halo(cells, sides, width):
    for axis, dim in sides:
        count = lax.axis_size(axis)
        ends = count - 1
        head = lax.slice_in_dim(cells, 0, width, axis=dim)
        tail = lax.slice_in_dim(cells, cells.shape[dim] - width, cells.shape[dim], axis=dim)
        cells = jnp.concatenate(
            [
                lax.ppermute(tail, axis, [(i, (i + 1) % count) for i in range(ends)]),
                cells,
                lax.ppermute(head, axis, [((i + 1) % count, i) for i in range(ends)]),
            ],
            axis=dim,
        )
    return cells


def lift_inputs(noisy, condition, present, level, lift_weight, level_weight):
    state = lift_weight[0][None, :, None, None] * noisy[:, None]
    state = state + lift_weight[1][None, :, None, None] * condition[:, None]
    state = state + lift_weight[2][None, :, None, None] * present[:, None, None, :]
    return state + level[:, None, None, None] * level_weight[None, :, None, None]


def normalize(state, gain):
    mean_square = jnp.mean(state * state, axis=1, keepdims=True)
    return state * lax.rsqrt(mean_square + 1e-05) * gain[None, :, None, None]


def conv_layer(padded, kernel, dilation):
    widened = jnp.pad(padded, ((0, 0), (0, 0), (0, 0), (DMAX, DMAX)))
    length = padded.shape[2] - 2 * DMAX
    columns = padded.shape[3]
    tap_list = []
    for row_tap in range(3):
        for col_tap in range(3):
            time_start = DMAX + (row_tap - 1) * dilation
            recv_start = DMAX + (col_tap - 1) * dilation
            window = lax.dynamic_slice_in_dim(widened, time_start, length, 2)
            window = lax.dynamic_slice_in_dim(window, recv_start, columns, 3)
            tap_list.append(window)
    stacked = jnp.stack(tap_list, 0)
    return jnp.einsum("kscyx,kco->soyx", stacked, kernel, preferred_element_type=jnp.float32)


def block_update(normed, kernel, projection, dilation):
    summed = conv_layer(normed, kernel, dilation)
    activated = jax.nn.gelu(summed).astype(jnp.bfloat16)
    return jnp.einsum("soyx,oc->scyx", activated, projection, preferred_element_type=jnp.float32)


def per_device(
    noisy_gather,
    observed,
    missing,
    noise_level,
    dilations,
    lift_weight,
    level_weight,
    norm_gain,
    conv_weight,
    out_weight,
    head_weight,
):
    steps_dev = noisy_gather.shape[1]
    receivers = noisy_gather.shape[2]
    total_time = steps_dev * lax.axis_size("tm")
    shot_rows = lax.all_to_all(observed, "shot", split_axis=0, concat_axis=2, tiled=True)
    present = (1 - missing).astype(jnp.float32)
    masked = shot_rows * present[:, None, :]
    energy = lax.psum(jnp.sum(masked * masked, axis=(1, 2)), "tm")
    cond_scale = lax.rsqrt(energy / (total_time * receivers) + 1e-05)
    condition = masked * cond_scale[:, None, None]
    state = lift_inputs(noisy_gather, condition, present, noise_level, lift_weight, level_weight)
    for layer in range(LAYERS):
        normed = normalize(state, norm_gain[layer]).astype(jnp.bfloat16)
        padded = with_halo(normed, (("tm", 2),), DMAX)
        state = state + block_update(
            padded, conv_weight[layer], out_weight[layer], dilations[layer]
        )
    return jnp.einsum("scyx,c->syx", state, head_weight, precision=lax.Precision.HIGHEST)


def solution(mesh):
    in_specs = (
        P("shot", "tm", None),
        P(None, "tm", "shot"),
        P("shot", None),
        P("shot"),
        P(),
        P(),
        P(),
        P(),
        P(),
        P(),
        P(),
    )
    out_specs = P("shot", "tm", None)
    return jax.shard_map(
        per_device, mesh=mesh, in_specs=in_specs, out_specs=out_specs, check_vma=False
    )
```

profile of v0, /device:TPU:89, one launch (start us, length us, event | category | flops | bytes accessed | tf_op | source)
XLA Modules:
  0.0 221.5 jit_solution(17828210338721010997)
XLA Ops:
  0.0 1.7 reshape.122
  1.7 7.5 %all-to-all-start = ((f32[16,1,1024]{2,1,0:T(1,128)}), f32[16,1,1024]{2,1,0:T(1,128)S(1)}, u32[]{:S(2)}, u32[]{:S(2)}) async-start(f32[16,1,1024]{2,1,0:T(1,128)} %reshape.122), calls=%async_computation | async-start | bytes 131072 | tf_op jit(solution)/shard_map/all_to_all | solution.py:77
  9.2 0.7 subtract_convert_fusion
  9.9 0.8 slice_bitcast_fusion.4
  10.7 0.8 slice_bitcast_fusion
  11.5 0.7 broadcast_multiply_fusion.1
  12.2 2.3 %all-to-all-done = f32[16,1,1024]{2,1,0:T(1,128)S(1)} async-done(((f32[16,1,1024]{2,1,0:T(1,128)}), f32[16,1,1024]{2,1,0:T(1,128)S(1)}, u32[]{:S(2)}, u32[]{:S(2)}) %all-to-all-start) | async-done | bytes 65568 | tf_op jit(solution)/shard_map/all_to_all | solution.py:77
  15.0 0.8 reduce.1
  16.1 42.2 %psum.7 = f32[2]{0:T(128)S(1)} all-reduce(f32[2]{0:T(128)S(1)} %fusion.44), channel_id=1, replica_groups=mesh['shot'=16,'tm'=16] {'tm'}, use_global_device_ids=true, to_apply=%region_1.0 | all-reduce | flops 2 | bytes 16 | tf_op jit(solution)/shard_map/psum | solution.py:80
  58.5 2.6 %multiply_reduce_fusion.1 = f32[2,64,128]{2,1,0:T(8,128)S(1)} fusion(f32[2,64]{1,0:T(2,128)S(1)} %broadcast_multiply_fusion.1, f32[2,64,128]{2,1,0:T(8,128)S(1)} %get-tuple-element.15, f32[2,64,128]{2,1,0:T(8,128)S(1)} %get-tuple-element.14, f32[64]{0:T(128)S(1)} %get-tuple-element.11, f32[2,64,128]{2,1,0:T(8,128)} %param.11, f32[64]{0:T(128)S(1)} %get-tuple-element.9), kind=kLoop, calls=%fused_computation.39 | loop fusion | flops 7323648 | bytes 263168 | tf_op jit(solution)/shard_map/reduce_sum | solution.py:35
  61.2 2.1 multiply_convert_fusion.2
  63.4 1.0 fusion.59
  64.4 10.2 %collective-permute-start = (bf16[2,64,16,128]{3,1,2,0:T(8,128)(2,1)}, bf16[2,64,16,128]{3,1,2,0:T(8,128)(2,1)S(1)}, u32[]{:S(2)}, u32[]{:S(2)}) collective-permute-start(bf16[2,64,16,128]{3,1,2,0:T(8,128)(2,1)} %get-tuple-element.7), channel_id=1, source_target_pairs={{0,1},{1,2},{2,3},{3,4},{4,5},{5,6},{6,7},{7,8},{8,9},{9,10},{10,1... | collective-permute-start | bytes 1572872 | tf_op jit(solution)/shard_map/ppermute | solution.py:18
  74.6 2.2 collective-permute-start.1
  76.8 0.6 fusion.60
  80.0 6.6 %collective-permute-done = bf16[2,64,16,128]{3,1,2,0:T(8,128)(2,1)S(1)} collective-permute-done((bf16[2,64,16,128]{3,1,2,0:T(8,128)(2,1)}, bf16[2,64,16,128]{3,1,2,0:T(8,128)(2,1)S(1)}, u32[]{:S(2)}, u32[]{:S(2)}) %collective-permute-start) | collective-permute-done | bytes 524320 | tf_op jit(solution)/shard_map/ppermute | solution.py:18
  86.6 10.3 %collective-permute-done.1 = bf16[2,64,16,128]{3,1,2,0:T(8,128)(2,1)S(1)} collective-permute-done((bf16[2,64,16,128]{3,1,2,0:T(8,128)(2,1)}, bf16[2,64,16,128]{3,1,2,0:T(8,128)(2,1)S(1)}, u32[]{:S(2)}, u32[]{:S(2)}) %collective-permute-start.1) | collective-permute-done | bytes 524320 | tf_op jit(solution)/shard_map/ppermute | solution.py:20
  97.0 7.3 %select_maximum_fusion.2 = bf16[2,64,96,160]{3,1,2,0:T(8,128)(2,1)S(1)} fusion(bf16[2,64,16,128]{3,1,2,0:T(8,128)(2,1)S(1)} %collective-permute-done.1, bf16[2,64,64,128]{3,1,2,0:T(8,128)(2,1)S(1)} %multiply_convert_fusion.2, bf16[2,64,16,128]{3,1,2,0:T(8,128)(2,1)S(1)} %collective-permute-done), kind=kLoop, calls=%fused_computation.29 | loop fusion | flops 23592960 | bytes 7077888 | tf_op jit(solution)/shard_map/concatenate | solution.py:16
  104.2 0.6 dynamic_slice.110
  104.8 2.2 bitcast_dynamic-update-slice_fusion.12
  107.0 2.2 %fusion.36 = bf16[9,2,64,64,128]{4,2,0,3,1:T(8,128)(2,1)} fusion(bf16[9,2,64,64,128]{4,2,0,3,1:T(8,128)(2,1)} %bitcast_dynamic-update-slice_fusion.12, bf16[2,64,96,160]{3,1,2,0:T(8,128)(2,1)S(1)} %select_maximum_fusion.2, s32[]{:T(128)S(6)} %select_n.56, s32[]{:T(128)S(6)} %add.286), kind=kLoop, calls=%fused_computation.49 | loop fusion | bytes 4194312
  109.2 2.2 %bitcast_dynamic-update-slice_fusion.11 = bf16[9,2,64,64,128]{4,2,0,3,1:T(8,128)(2,1)} fusion(bf16[9,2,64,64,128]{4,2,0,3,1:T(8,128)(2,1)} %fusion.36, bf16[2,64,96,160]{3,1,2,0:T(8,128)(2,1)S(1)} %select_maximum_fusion.2, s32[]{:T(128)S(6)} %select_n.57, s32[]{:T(128)S(6)} %select_n.61), kind=kLoop, calls=%fused_computation.61 | loop fusion | bytes 4194312
  111.5 2.2 %bitcast_dynamic-update-slice_fusion.10 = bf16[9,2,64,64,128]{4,2,0,3,1:T(8,128)(2,1)} fusion(bf16[9,2,64,64,128]{4,2,0,3,1:T(8,128)(2,1)} %bitcast_dynamic-update-slice_fusion.11, bf16[2,64,64,160]{3,1,2,0:T(8,128)(2,1)S(1)} %dynamic_slice.110, s32[]{:T(128)S(6)} %select_n.58), kind=kLoop, calls=%fused_computation.60 | loop fusion | bytes 4194308
  113.7 2.6 %fusion.32 = bf16[9,2,64,64,128]{4,2,0,3,1:T(8,128)(2,1)} fusion(bf16[9,2,64,64,128]{4,2,0,3,1:T(8,128)(2,1)} %bitcast_dynamic-update-slice_fusion.10, f32[64]{0:T(128)S(1)} %get-tuple-element.13, f32[2,64,128]{2,1,0:T(8,128)S(1)} %add_rsqrt_fusion.1, f32[2,64]{1,0:T(2,128)S(1)} %broadcast_multiply_fusion.1, f32[2,64,128]{2,1,0:T(8,128)S(1)} %get-tuple-element.15, ...), kind=kLoop, calls=%fused_computation.41 | loop fusion | flops 8388608 | bytes 2360576
  116.3 2.2 bitcast_dynamic-update-slice_fusion.9
  118.6 2.2 bitcast_dynamic-update-slice_fusion.8
  120.7 2.2 %fusion.35 = bf16[9,2,64,64,128]{4,2,0,3,1:T(8,128)(2,1)} fusion(bf16[9,2,64,64,128]{4,2,0,3,1:T(8,128)(2,1)} %bitcast_dynamic-update-slice_fusion.8, bf16[2,64,96,160]{3,1,2,0:T(8,128)(2,1)S(1)} %select_maximum_fusion.2, s32[]{:T(128)S(6)} %select_n.62, s32[]{:T(128)S(6)} %add.286), kind=kLoop, calls=%fused_computation.47 | loop fusion | bytes 4194312
  123.0 2.2 %bitcast_dynamic-update-slice_fusion.7 = bf16[9,2,64,64,128]{4,2,0,3,1:T(8,128)(2,1)} fusion(bf16[9,2,64,64,128]{4,2,0,3,1:T(8,128)(2,1)} %fusion.35, bf16[2,64,96,160]{3,1,2,0:T(8,128)(2,1)S(1)} %select_maximum_fusion.2, s32[]{:T(128)S(6)} %select_n.63, s32[]{:T(128)S(6)} %select_n.61), kind=kLoop, calls=%fused_computation.57 | loop fusion | bytes 4194312 | tf_op jit(solution)/shard_map/stack | solution.py:51
  125.2 17.6 %multiply_reduce_fusion = (f32[2,64,128]{2,1,0:T(8,128)S(1)}, f32[2,64,64,128]{3,1,2,0:T(8,128)}) fusion(bf16[2,256,64]{1,2,0:T(8,128)(2,1)S(1)} %copy-done.6, bf16[9,2,64,64,128]{4,2,0,3,1:T(8,128)(2,1)} %bitcast_dynamic-update-slice_fusion.7, bf16[2,9,64,256]{3,2,1,0:T(8,128)(2,1)S(1)} %copy-done.3, f32[2,64]{1,0:T(2,128)S(1)} %broadcast_multiply_fusion.1, ...), kind=kOutput, calls=%fused_computation.36 | convolution fusion | flops 5414830080 | bytes 23660544 | tf_op jit(solution)/shard_map/soyx,oc->scyx/dot_general | solution.py:58
  142.9 3.1 %multiply_convert_fusion = bf16[2,64,64,128]{3,1,2,0:T(8,128)(2,1)S(1)} fusion(f32[2,64,64,128]{3,1,2,0:T(8,128)} %get-tuple-element.19, f32[64]{0:T(128)S(1)} %get-tuple-element.12, f32[2,64,128]{2,1,0:T(8,128)S(1)} %add_rsqrt_fusion), kind=kLoop, calls=%fused_computation.35 | loop fusion | flops 3145728 | bytes 6357248 | tf_op jit(solution)/shard_map/convert_element_type | solution.py:85
  145.9 1.0 fusion.58
  147.0 1.9 collective-permute-start.2
  148.9 2.4 %collective-permute-start.3 = (bf16[2,64,16,128]{3,1,2,0:T(8,128)(2,1)}, bf16[2,64,16,128]{3,1,2,0:T(8,128)(2,1)S(1)}, u32[]{:S(2)}, u32[]{:S(2)}) collective-permute-start(bf16[2,64,16,128]{3,1,2,0:T(8,128)(2,1)} %get-tuple-element.6), channel_id=1, source_target_pairs={{1,0},{2,1},{3,2},{4,3},{5,4},{6,5},{7,6},{8,7},{9,8},{10,9},{11,1... | collective-permute-start | bytes 1572872 | tf_op jit(solution)/shard_map/ppermute | solution.py:20
  153.9 3.0 %collective-permute-done.2 = bf16[2,64,16,128]{3,1,2,0:T(8,128)(2,1)S(1)} collective-permute-done((bf16[2,64,16,128]{3,1,2,0:T(8,128)(2,1)}, bf16[2,64,16,128]{3,1,2,0:T(8,128)(2,1)S(1)}, u32[]{:S(2)}, u32[]{:S(2)}) %collective-permute-start.2) | collective-permute-done | bytes 524320 | tf_op jit(solution)/shard_map/ppermute | solution.py:18
  156.9 10.3 %collective-permute-done.3 = bf16[2,64,16,128]{3,1,2,0:T(8,128)(2,1)S(1)} collective-permute-done((bf16[2,64,16,128]{3,1,2,0:T(8,128)(2,1)}, bf16[2,64,16,128]{3,1,2,0:T(8,128)(2,1)S(1)}, u32[]{:S(2)}, u32[]{:S(2)}) %collective-permute-start.3) | collective-permute-done | bytes 524320 | tf_op jit(solution)/shard_map/ppermute | solution.py:20
  167.2 7.4 %select_maximum_fusion = bf16[2,64,96,160]{3,1,2,0:T(8,128)(2,1)S(1)} fusion(bf16[2,64,16,128]{3,1,2,0:T(8,128)(2,1)S(1)} %collective-permute-done.3, bf16[2,64,64,128]{3,1,2,0:T(8,128)(2,1)S(1)} %multiply_convert_fusion, bf16[2,64,16,128]{3,1,2,0:T(8,128)(2,1)S(1)} %collective-permute-done.2), kind=kLoop, calls=%fused_computation.27 | loop fusion | flops 23592960 | bytes 7077888 | tf_op jit(solution)/shard_map/concatenate | solution.py:16
  175.2 2.2 bitcast_dynamic-update-slice_fusion.6
  177.4 2.1 fusion.34
  179.6 2.2 bitcast_dynamic-update-slice_fusion.5
  181.7 2.2 bitcast_dynamic-update-slice_fusion.4
  183.9 2.2 %bitcast_dynamic-update-slice_fusion.3 = bf16[9,2,64,64,128]{4,2,3,1,0:T(8,128)(2,1)} fusion(bf16[9,2,64,64,128]{4,2,3,1,0:T(8,128)(2,1)} %bitcast_dynamic-update-slice_fusion.4, f32[64]{0:T(128)S(1)} %get-tuple-element.12, f32[2,64,64,128]{3,1,2,0:T(8,128)S(1)} %copy-done.1, f32[2,64,128]{2,1,0:T(8,128)S(1)} %add_rsqrt_fusion), kind=kLoop, calls=%fused_computation.53 | loop fusion | flops 3145728 | bytes 6357248
  186.2 2.2 bitcast_dynamic-update-slice_fusion.2
  188.3 2.2 bitcast_dynamic-update-slice_fusion.1
  190.5 2.2 fusion.33
  192.7 2.2 bitcast_dynamic-update-slice_fusion
  194.8 14.2 %fusion.19 = f32[2,64,128,256]{3,2,0,1:T(8,128)} fusion(bf16[9,2,64,64,128]{4,2,3,1,0:T(8,128)(2,1)} %bitcast_dynamic-update-slice_fusion, bf16[2,9,64,256]{3,2,1,0:T(8,128)(2,1)S(1)} %copy-done.4), kind=kOutput, calls=%fused_computation.23 | convolution fusion | flops 4831838208 | bytes 35946496 | tf_op jit(solution)/shard_map/kscyx,kco->soyx/dot_general | solution.py:52
  209.0 9.2 %fusion.26 = f32[2,64,128,64]{2,3,1,0:T(8,128)S(1)} fusion(f32[2,64,128,256]{3,2,0,1:T(8,128)} %fusion.19, bf16[2,256,64]{1,2,0:T(8,128)(2,1)S(1)} %copy-done.6), kind=kOutput, calls=%fused_computation.26 | convolution fusion | flops 574619648 | bytes 21004288 | tf_op jit(solution)/shard_map/soyx,oc->scyx/dot_general | solution.py:58
  218.2 3.1 %fusion.29 = f32[1,2,64,128]{3,0,2,1:T(1,128)} fusion(f32[2,64,64,128]{3,1,2,0:T(8,128)S(1)} %copy-done.1, f32[2,64,128,64]{2,3,1,0:T(8,128)S(1)} %fusion.26, f32[64]{0:T(128)S(1)} %copy-done), kind=kOutput, calls=%fused_computation.33 | convolution fusion | flops 13631488 | bytes 8454400 | tf_op jit(solution)/shard_map/scyx,c->syx/dot_general | solution.py:90
  (25 shorter events, 1.7 us)
Async XLA Ops:
  0.0 218.2 %copy-start = (f32[64]{0:T(128)S(1)}, f32[64]{0:T(128)}, u32[]{:S(2)}) copy-start(f32[64]{0:T(128)} %param.21) | copy-start | bytes 772
  0.0 76.8 %copy-start.5 = (s32[2]{0:T(128)S(1)}, s32[2]{0:T(128)}, u32[]{:S(2)}) copy-start(s32[2]{0:T(128)} %param.15) | copy-start | bytes 28
  1.7 12.8 %all-to-all-start = ((f32[16,1,1024]{2,1,0:T(1,128)}), f32[16,1,1024]{2,1,0:T(1,128)S(1)}, u32[]{:S(2)}, u32[]{:S(2)}) async-start(f32[16,1,1024]{2,1,0:T(1,128)} %reshape.122), calls=%async_computation | async-start | bytes 131072 | tf_op jit(solution)/shard_map/all_to_all | solution.py:77
  64.4 22.2 %collective-permute-start = (bf16[2,64,16,128]{3,1,2,0:T(8,128)(2,1)}, bf16[2,64,16,128]{3,1,2,0:T(8,128)(2,1)S(1)}, u32[]{:S(2)}, u32[]{:S(2)}) collective-permute-start(bf16[2,64,16,128]{3,1,2,0:T(8,128)(2,1)} %get-tuple-element.7), channel_id=1, source_target_pairs={{0,1},{1,2},{2,3},{3,4},{4,5},{5,6},{6,7},{7,8},{8,9},{9,10},{10,1... | collective-permute-start | bytes 1572872 | tf_op jit(solution)/shard_map/ppermute | solution.py:18
  74.6 22.3 %collective-permute-start.1 = (bf16[2,64,16,128]{3,1,2,0:T(8,128)(2,1)}, bf16[2,64,16,128]{3,1,2,0:T(8,128)(2,1)S(1)}, u32[]{:S(2)}, u32[]{:S(2)}) collective-permute-start(bf16[2,64,16,128]{3,1,2,0:T(8,128)(2,1)} %get-tuple-element.8), channel_id=1, source_target_pairs={{1,0},{2,1},{3,2},{4,3},{5,4},{6,5},{7,6},{8,7},{9,8},{10,9},{11,1... | collective-permute-start | bytes 1572872 | tf_op jit(solution)/shard_map/ppermute | solution.py:20
  107.0 6.7 %copy-start.2 = (f32[2,64,128]{2,1,0:T(8,128)S(1)}, f32[2,64,128]{2,1,0:T(8,128)}, u32[]{:S(2)}) copy-start(f32[2,64,128]{2,1,0:T(8,128)} %param.11) | copy-start | bytes 196612
  118.6 6.6 %copy-start.3 = (bf16[2,9,64,256]{3,2,1,0:T(8,128)(2,1)S(1)}, bf16[2,9,64,256]{3,2,1,0:T(8,128)(2,1)}, u32[]{:S(2)}) copy-start(bf16[2,9,64,256]{3,2,1,0:T(8,128)(2,1)} %param.19) | copy-start | bytes 1769476
  118.6 6.6 %copy-start.6 = (bf16[2,256,64]{1,2,0:T(8,128)(2,1)S(1)}, bf16[2,256,64]{1,2,0:T(8,128)(2,1)}, u32[]{:S(2)}) copy-start(bf16[2,256,64]{1,2,0:T(8,128)(2,1)} %param.20) | copy-start | bytes 196612
  147.0 9.9 %collective-permute-start.2 = (bf16[2,64,16,128]{3,1,2,0:T(8,128)(2,1)}, bf16[2,64,16,128]{3,1,2,0:T(8,128)(2,1)S(1)}, u32[]{:S(2)}, u32[]{:S(2)}) collective-permute-start(bf16[2,64,16,128]{3,1,2,0:T(8,128)(2,1)} %get-tuple-element.5), channel_id=1, source_target_pairs={{0,1},{1,2},{2,3},{3,4},{4,5},{5,6},{6,7},{7,8},{8,9},{9,10},{10,1... | collective-permute-start | bytes 1572872 | tf_op jit(solution)/shard_map/ppermute | solution.py:18
  148.9 18.3 %collective-permute-start.3 = (bf16[2,64,16,128]{3,1,2,0:T(8,128)(2,1)}, bf16[2,64,16,128]{3,1,2,0:T(8,128)(2,1)S(1)}, u32[]{:S(2)}, u32[]{:S(2)}) collective-permute-start(bf16[2,64,16,128]{3,1,2,0:T(8,128)(2,1)} %get-tuple-element.6), channel_id=1, source_target_pairs={{1,0},{2,1},{3,2},{4,3},{5,4},{6,5},{7,6},{8,7},{9,8},{10,9},{11,1... | collective-permute-start | bytes 1572872 | tf_op jit(solution)/shard_map/ppermute | solution.py:20
  177.4 6.5 %copy-start.1 = (f32[2,64,64,128]{3,1,2,0:T(8,128)S(1)}, f32[2,64,64,128]{3,1,2,0:T(8,128)}, u32[]{:S(2)}) copy-start(f32[2,64,64,128]{3,1,2,0:T(8,128)} %get-tuple-element.19) | copy-start | bytes 12582916
  188.3 6.5 %copy-start.4 = (bf16[2,9,64,256]{3,2,1,0:T(8,128)(2,1)S(1)}, bf16[2,9,64,256]{3,2,1,0:T(8,128)(2,1)}, u32[]{:S(2)}) copy-start(bf16[2,9,64,256]{3,2,1,0:T(8,128)(2,1)} %param.19) | copy-start | bytes 1769476
where the time goes:
time: 226 us; the launch traced here: 222 us
  matrix products  44.1 us (20%)
  local copies, waits for them, and re-layouts  43 us (19%)
  blocking collectives  42.2 us (19%)
  waiting for transfers between devices  32.5 us (14%)
  other arithmetic  29.9 us (13%)
  starting transfers between devices  24.2 us (11%)
  between operations  5.59 us (2%)
    psum x1, blocking collectives, per_device(): energy = lax.psum(jnp.sum(masked * masked, axis=(1, 2)), 'tm')  42.2 us
    unnamed x30, local copies, waits for them, and re-layouts  32.5 us
    dot_general x2, matrix products, block_update(): jnp.einsum('soyx,oc->scyx', activated, projection, preferred_element_type...  26.8 us
    ppermute x2, waiting for transfers between devices, with_halo(): lax.ppermute(head, axis, [((i + 1) % count, i) for i in range(ends)])  20.6 us
    concatenate x2, other arithmetic, with_halo(): jnp.concatenate([lax.ppermute(tail, axis, [(i, (i + 1) % count) for i in...  14.7 us
    dot_general x1, matrix products, conv_layer(): jnp.einsum('kscyx,kco->soyx', stacked, kernel, preferred_element_type=jnp...  14.2 us
    ppermute x2, starting transfers between devices, with_halo(): lax.ppermute(tail, axis, [(i, (i + 1) % count) for i in range(ends)])  12.1 us
    ppermute x2, waiting for transfers between devices, with_halo(): lax.ppermute(tail, axis, [(i, (i + 1) % count) for i in range(ends)])  9.6 us
  transfers between devices with their start and end apart: 5, of which 5 were waited for; matrix products, arithmetic and copies ran while one was open for 2% of the time, Pallas kernels for 0%

commit v1 on v0

v1 whole, which is shorter than its diff:
```python
import jax
import jax.numpy as jnp
from jax import lax
from jax.experimental import pallas as pl
from jax.experimental.pallas import tpu as pltpu
from jax.sharding import PartitionSpec as P

MESH = pl.DeviceIdType.MESH
DMAX = 16
HALO = 2 * DMAX
TANH_SCALE = 0.7978845608028654
TANH_CUBE = 0.044715
UNROLL = 4


def comm_kernel(
    shots, spans, obs, noisy, missing, obs_ext, noisy_ext, energy,
    landed, sums, sent, shot_send, shot_recv, halo_send, halo_recv, sum_send, sum_recv,
):
    me_shot = lax.axis_index("shot")
    me_tm = lax.axis_index("tm")
    steps = noisy.shape[1]
    barrier = pltpu.get_barrier_semaphore()
    for step in range(1, shots):
        pl.semaphore_signal(
            barrier, inc=1, device_id={"shot": lax.rem(me_shot + step, shots)}, device_id_type=MESH
        )
    for step in range(1, spans):
        pl.semaphore_signal(
            barrier, inc=1, device_id={"tm": lax.rem(me_tm + step, spans)}, device_id_type=MESH
        )
    pl.semaphore_wait(barrier, shots + spans - 2)

    right = {"tm": lax.rem(me_tm + 1, spans)}
    left = {"tm": lax.rem(me_tm + spans - 1, spans)}

    def halo(source, first, target, slot):
        up = pltpu.make_async_remote_copy(
            src_ref=source.at[:, pl.ds(first + steps - HALO, HALO), :],
            dst_ref=target.at[:, pl.ds(0, HALO), :],
            send_sem=halo_send.at[slot], recv_sem=halo_recv.at[slot],
            device_id=right, device_id_type=MESH,
        )
        down = pltpu.make_async_remote_copy(
            src_ref=source.at[:, pl.ds(first, HALO), :],
            dst_ref=target.at[:, pl.ds(HALO + steps, HALO), :],
            send_sem=halo_send.at[slot + 1], recv_sem=halo_recv.at[slot + 1],
            device_id=left, device_id_type=MESH,
        )
        up.start()
        down.start()
        return [up, down]

    exchange = []
    for step in range(1, shots):
        other = lax.rem(me_shot + step, shots)
        copy = pltpu.make_async_remote_copy(
            src_ref=obs.at[pl.ds(2 * other, 2)], dst_ref=landed.at[me_shot],
            send_sem=shot_send.at[step], recv_sem=shot_recv.at[step],
            device_id={"shot": other}, device_id_type=MESH,
        )
        copy.start()
        exchange.append(copy)
    halos = halo(noisy, 0, noisy_ext, 0)
    landed[me_shot] = obs[pl.ds(2 * me_shot, 2)]
    noisy_ext[:, HALO : HALO + steps, :] = noisy[...]
    for copy in exchange:
        copy.wait_recv()
    rows = jnp.stack([landed[:, s].reshape(8 * shots, steps).T for s in range(2)])
    obs_ext[:, HALO : HALO + steps, :] = rows
    halos += halo(obs_ext, HALO, obs_ext, 2)
    masked = rows * (1 - missing[...]).astype(jnp.float32)[:, None, :]
    sent[...] = jnp.sum(masked * masked, axis=1)
    sharing = []
    for step in range(1, spans):
        other = lax.rem(me_tm + step, spans)
        copy = pltpu.make_async_remote_copy(
            src_ref=sent, dst_ref=sums.at[me_tm],
            send_sem=sum_send.at[step], recv_sem=sum_recv.at[step],
            device_id={"tm": other}, device_id_type=MESH,
        )
        copy.start()
        sharing.append(copy)
    sums[me_tm] = sent[...]
    for copy in sharing:
        copy.wait_recv()
    total = jnp.sum(sums[...], axis=0)
    energy[...] = jnp.broadcast_to(jnp.sum(total, axis=1, keepdims=True), energy.shape)
    for copy in exchange + sharing:
        copy.wait_send()
    for copy in halos:
        copy.wait()


def exchange_inputs(shots, spans, obs, noisy, missing):
    steps = noisy.shape[1]
    vm = pl.BlockSpec(memory_space=pltpu.VMEM)
    ext = jax.ShapeDtypeStruct((2, steps + 2 * HALO, 8 * shots), jnp.float32)
    dma = pltpu.SemaphoreType.DMA
    return pl.pallas_call(
        lambda *refs: comm_kernel(shots, spans, *refs),
        out_shape=(ext, ext, jax.ShapeDtypeStruct((2, 128), jnp.float32)),
        in_specs=[vm] * 3,
        out_specs=(vm,) * 3,
        scratch_shapes=[
            pltpu.VMEM((shots, 2, 8, steps), jnp.float32),
            pltpu.VMEM((spans, 2, 128), jnp.float32),
            pltpu.VMEM((2, 128), jnp.float32),
            dma((shots,)), dma((shots,)), dma((4,)), dma((4,)), dma((spans,)), dma((spans,)),
        ],
        compiler_params=pltpu.CompilerParams(
            collective_id=0, has_side_effects=True, vmem_limit_bytes=32 * 2**20
        ),
        name="exchange",
    )(obs, noisy, missing)


def gelu_of_half(h):
    u = h * (2 * TANH_SCALE + (8 * TANH_SCALE * TANH_CUBE) * (h * h))
    return (h + h * jnp.tanh(u)).astype(jnp.bfloat16)


def mm(a, b):
    return jnp.dot(a, b, preferred_element_type=jnp.float32)


def column(row):
    return jnp.broadcast_to(jnp.broadcast_to(row, (8, row.shape[1])).T[:, :1], (row.shape[1], 128))


def compute_kernel(
    spans, dil, level, energy, noisy, obs, missing, lift, levw, gain, cw, ow, head, out,
    x1, x2, state, wt, owt, lw,
):
    f32, bf16 = jnp.float32, jnp.bfloat16
    steps = out.shape[1]
    total_time = spans * steps
    d1, d2 = dil[0], dil[1]
    first = lax.axis_index("tm") * steps - HALO

    for l in range(2):
        parts = [[], [], [], []]
        for j in range(3):
            w0, w1, w2 = [cw[l, 3 * i + j].astype(f32) * 0.5 for i in range(3)]
            outer = (w0 + w2) * 0.5
            parts[0].append(w0)
            parts[1].append(outer + w1 * 0.5)
            parts[2].append(outer - w1 * 0.5)
            parts[3].append(w2)
        for k in range(4):
            wt[l, k] = jnp.concatenate(parts[k], 0).T.astype(bf16)
    owt[...] = ow[0]
    head_row = head[...]
    last = lax.dot_general(
        head_row, ow[1].astype(f32), (((1,), (0,)), ((), ())), precision=lax.Precision.HIGHEST
    )
    last_high = last.astype(bf16)
    last_low = (last - last_high.astype(f32)).astype(bf16)
    last_rows = jnp.concatenate([last_high, last_low, jnp.zeros((14, 256), bf16)], 0)
    lane = lax.broadcasted_iota(jnp.int32, (64, 128), 1)

    lw[0] = column(lift[0:1, :])
    lw[1] = column(lift[1:2, :])
    scales = []
    for s in range(2):
        present = (1 - missing[s : s + 1, :]).astype(f32)
        lw[2 + s] = column(lift[2:3, :]) * present + level[s] * column(levw[...])
        scales.append(present * lax.rsqrt(energy[s : s + 1, :] / (total_time * 128) + 1e-5))
    lw[4] = column(gain[0:1, :])
    lw[5] = column(gain[1:2, :])
    lw[6] = column(head_row)

    def put(ref, row, halves, d):
        ref[row, 64:128, :] = jnp.concatenate(halves, 1).astype(bf16)
        low = [jnp.where(lane >= d, pltpu.roll(a, d, 1), 0.0) for a in halves]
        ref[row, 0:64, :] = jnp.concatenate(low, 1).astype(bf16)
        high = [jnp.where(lane < 128 - d, pltpu.roll(a, 128 - d, 1), 0.0) for a in halves]
        ref[row, 128:192, :] = jnp.concatenate(high, 1).astype(bf16)

    def norm(a, g, row):
        time = row + first
        inside = jnp.where(jnp.logical_and(time >= 0, time < total_time), 1.0, 0.0).astype(f32)
        mean_square = jnp.sum(a * a, axis=0, keepdims=True) * (1.0 / 64)
        return a * (lax.rsqrt(mean_square + 1e-5) * inside) * g

    def lift_row(row):
        normed = []
        for s in range(2):
            a = lw[0] * noisy[s, pl.ds(row, 1), :]
            a = a + lw[1] * (obs[s, pl.ds(row, 1), :] * scales[s]) + lw[2 + s]
            state[row, :, s * 128 : (s + 1) * 128] = a
            normed.append(norm(a, lw[4], row))
        put(x1, row, normed, d1)

    def unrolled(count, body, by):
        def several(q, carry):
            for u in range(by):
                body(q * by + u)
            return carry

        lax.fori_loop(0, (count + by - 1) // by, several, 0)

    unrolled(steps + 2 * (d1 + d2), lambda i: lift_row(HALO - d1 - d2 + i), 4)

    def conv_pair(l, ref, r, d, then):
        a0, a1, a2, a3 = ref[r - d], ref[r], ref[r + d], ref[r + 2 * d]
        m1 = mm(wt[l, 1], a1 + a2)
        m2 = mm(wt[l, 2], a2 - a1)
        m0 = mm(wt[l, 0], a0 - a2)
        m3 = mm(wt[l, 3], a1 - a3)
        then(0, gelu_of_half(m0 + (m1 + m2)))
        then(1, gelu_of_half((m1 - m2) - m3))

    def pair_row(p, d):
        block = p // d
        return block * (2 * d) + (p - block * d)

    rows = steps + 2 * d2
    whole = rows // (2 * d1)
    pairs = whole * d1 + jnp.minimum(rows - whole * 2 * d1, d1)

    def first_pair(p):
        r0 = pair_row(p, d1) + HALO - d2

        def then(e, act):
            r = r0 + e * d1
            updated = state[r] + mm(owt[...], act)
            state[r] = updated
            put(x2, r - DMAX, [norm(updated[:, s * 128 : (s + 1) * 128], lw[5], r) for s in range(2)], d2)

        conv_pair(0, x1, r0, d1, then)

    unrolled(pairs, first_pair, UNROLL)

    def second_pair(p):
        r0 = pair_row(p, d2)

        def then(e, act):
            r = r0 + e * d2
            y = mm(last_rows, act)
            y = y[0:1, :] + y[1:2, :]
            for s in range(2):
                lanes = slice(s * 128, (s + 1) * 128)
                h = jnp.sum(state[r + HALO, :, lanes] * lw[6], axis=0, keepdims=True)
                out[s, pl.ds(r, 1), :] = h + y[:, lanes]

        conv_pair(1, x2, r0 + DMAX, d2, then)

    unrolled(steps // 2, second_pair, UNROLL)


def denoise(spans, dil, level, energy, noisy, obs, missing, lift, levw, gain, cw, ow, head):
    steps = noisy.shape[1] - 2 * HALO
    sm = pl.BlockSpec(memory_space=pltpu.SMEM)
    vm = pl.BlockSpec(memory_space=pltpu.VMEM)
    return pl.pallas_call(
        lambda *refs: compute_kernel(spans, *refs),
        out_shape=jax.ShapeDtypeStruct((2, steps, 128), jnp.float32),
        in_specs=[sm, sm] + [vm] * 10,
        out_specs=vm,
        scratch_shapes=[
            pltpu.VMEM((160, 192, 256), jnp.bfloat16),
            pltpu.VMEM((128, 192, 256), jnp.bfloat16),
            pltpu.VMEM((160, 64, 256), jnp.float32),
            pltpu.VMEM((2, 4, 256, 192), jnp.bfloat16),
            pltpu.VMEM((64, 256), jnp.bfloat16),
            pltpu.VMEM((7, 64, 128), jnp.float32),
        ],
        compiler_params=pltpu.CompilerParams(vmem_limit_bytes=50 * 2**20),
        name="denoise",
    )(dil, level, energy, noisy, obs, missing, lift, levw, gain, cw, ow, head)


def solution(mesh):
    shots, spans = mesh.shape["shot"], mesh.shape["tm"]

    def per_device(
        noisy_gather, observed, missing, noise_level, dilations, lift_weight, level_weight,
        norm_gain, conv_weight, out_weight, head_weight,
    ):
        obs_ext, noisy_ext, energy = exchange_inputs(shots, spans, jnp.swapaxes(observed, 1, 2), noisy_gather, missing)
        return denoise(
            spans, dilations, noise_level, energy, noisy_ext, obs_ext, missing, lift_weight,
            level_weight[None, :], norm_gain, conv_weight, jnp.swapaxes(out_weight, 1, 2), head_weight[None, :],
        )

    return jax.shard_map(
        per_device,
        mesh=mesh,
        in_specs=(
            P("shot", "tm", None), P(None, "tm", "shot"), P("shot", None), P("shot"),
            P(), P(), P(), P(), P(), P(), P(),
        ),
        out_specs=P("shot", "tm", None),
        check_vma=False,
    )
```

time: 226 us -> 70.6 us (0.31)
  the two profiles are of different devices: /device:TPU:89 before, /device:TPU:1 now
where the time goes in v1:
time: 70.6 us; the launch traced here: 70.4 us
  Pallas kernels  66.1 us (94%)
  local copies, waits for them, and re-layouts  4.18 us (6%)
    pallas_call x1, Pallas kernels, denoise(): pl.pallas_call(lambda *refs: compute_kernel(spans, *refs), out_shape=jax....  43.5 us
    pallas_call x1, Pallas kernels, exchange_inputs(): pl.pallas_call(lambda *refs: comm_kernel(shots, spans, *refs), out_shape=...  22.6 us
    unnamed x22, local copies, waits for them, and re-layouts  4.18 us

profile of v1, /device:TPU:1, one launch (start us, length us, event | category | flops | bytes accessed | tf_op | source)
XLA Modules:
  0.0 70.4 jit_solution(7703943083383457049)
XLA Ops:
  0.0 0.0 copy-start.4
  0.0 0.7 copy-done.4
  0.7 0.0 copy-start.1
  0.7 0.9 %copy-done.1 = f32[32,64,8]{1,2,0:T(8,128)S(1)} copy-done((f32[32,64,8]{1,2,0:T(8,128)S(1)}, f32[32,64,8]{1,2,0:T(8,128)}, u32[]{:S(2)}) %copy-start.1) | copy-done | bytes 65560
  1.6 0.0 copy-start.2
  1.6 0.8 %copy-done.2 = f32[2,64,128]{2,1,0:T(8,128)S(1)} copy-done((f32[2,64,128]{2,1,0:T(8,128)S(1)}, f32[2,64,128]{2,1,0:T(8,128)}, u32[]{:S(2)}) %copy-start.2) | copy-done | bytes 65560
  2.4 0.0 copy-start.3
  2.4 22.6 %exchange.1 = (f32[2,128,128]{2,1,0:T(8,128)S(1)}, f32[2,128,128]{2,1,0:T(8,128)S(1)}, f32[2,128]{1,0:T(2,128)S(1)}) custom-call(f32[32,8,64]{2,1,0:T(8,128)S(1)} %bitcast.4, f32[2,64,128]{2,1,0:T(8,128)S(1)} %copy-done.2, s32[2,128]{1,0:T(2,128)S(1)} %copy-done.4), custom_call_target="tpu_custom_call" | custom-call | tf_op jit(solution)/shard_map/exchange/pallas_call | solution.py:100
  25.0 0.0 copy-start.8
  25.1 0.0 copy-start.9
  25.1 0.0 copy-start.10
  25.1 0.0 copy-start.5
  25.1 0.0 copy-start.6
  25.1 0.0 copy-start.7
  25.1 0.0 copy-done.3
  25.1 0.6 copy-done.8
  25.7 0.0 copy-done.9
  25.7 0.0 copy-done.10
  25.7 0.0 copy-done.5
  25.8 0.0 copy-done.6
  25.8 0.0 copy-done.7
  25.8 0.0 copy-start
  25.8 1.1 %copy-done = bf16[2,9,64,256]{3,2,1,0:T(8,128)(2,1)S(1)} copy-done((bf16[2,9,64,256]{3,2,1,0:T(8,128)(2,1)S(1)}, bf16[2,9,64,256]{3,2,1,0:T(8,128)(2,1)}, u32[]{:S(2)}) %copy-start) | copy-done | bytes 589848
  26.9 43.5 %denoise.1 = f32[2,64,128]{2,1,0:T(8,128)} custom-call(s32[2]{0:T(128)S(1)} %copy-done.7, f32[2]{0:T(128)S(1)} %copy-done.8, f32[2,128]{1,0:T(2,128)S(1)} %get-tuple-element.8.refs_2_, f32[2,128,128]{2,1,0:T(8,128)S(1)} %get-tuple-element.9.refs_3_, f32[2,128,128]{2,1,0:T(8,128)S(1)} %get-tuple-element.10.refs_4_, s32[2,128]{1,0:T(2,128)S(1)} %copy-done.4, ...), custom_call_target="tpu_custom_call" | custom-call | tf_op jit(solution)/shard_map/denoise/pallas_call | solution.py:256
Async XLA Ops:
  0.0 0.7 copy-start.4
  0.7 0.9 %copy-start.1 = (f32[32,64,8]{1,2,0:T(8,128)S(1)}, f32[32,64,8]{1,2,0:T(8,128)}, u32[]{:S(2)}) copy-start(f32[32,64,8]{1,2,0:T(8,128)} %param.12) | copy-start | bytes 196612
  1.6 0.8 %copy-start.2 = (f32[2,64,128]{2,1,0:T(8,128)S(1)}, f32[2,64,128]{2,1,0:T(8,128)}, u32[]{:S(2)}) copy-start(f32[2,64,128]{2,1,0:T(8,128)} %refs_1_.2) | copy-start | bytes 196612
  2.4 22.7 %copy-start.3 = (bf16[2,256,64]{1,2,0:T(8,128)(2,1)S(1)}, bf16[2,256,64]{1,2,0:T(8,128)(2,1)}, u32[]{:S(2)}) copy-start(bf16[2,256,64]{1,2,0:T(8,128)(2,1)} %param.20) | copy-start | bytes 196612
  25.0 0.7 copy-start.8
  25.1 0.7 copy-start.9
  25.1 0.7 copy-start.10
  25.1 0.7 copy-start.5
  25.1 0.7 copy-start.6
  25.1 0.7 copy-start.7
  25.8 1.1 %copy-start = (bf16[2,9,64,256]{3,2,1,0:T(8,128)(2,1)S(1)}, bf16[2,9,64,256]{3,2,1,0:T(8,128)(2,1)}, u32[]{:S(2)}) copy-start(bf16[2,9,64,256]{3,2,1,0:T(8,128)(2,1)} %refs_9_.1) | copy-start | bytes 1769476

commit v2 on v1

v2 whole, which is shorter than its diff:
```python
import jax
import jax.numpy as jnp
from jax import lax
from jax.experimental import pallas as pl
from jax.experimental.pallas import tpu as pltpu
from jax.sharding import PartitionSpec as P

MESH = pl.DeviceIdType.MESH
DMAX = 16
HALO = 2 * DMAX
TANH_SCALE = 0.7978845608028654
TANH_CUBE = 0.044715
UNROLL = 8
f32, bf16 = jnp.float32, jnp.bfloat16


def column(row):
    return jnp.broadcast_to(jnp.broadcast_to(row, (8, row.shape[1])).T[:, :1], (row.shape[1], 128))


def exchange_kernel(
    shots, spans,
    obs, noisy, missing, level, dil, lift, levw, gain, cw, ow, head,
    masked_ext, noisy_ext, scale, cols, shot_base, wt, projection, last, dil_out,
    landed, sums, sent, miss, level_v, lift_v, levw_v, gain_v, cw_v, ow_v, head_v,
    local_sem, shot_send, shot_recv, halo_send, halo_recv, sum_send, sum_recv,
):
    me_shot = lax.axis_index("shot")
    me_tm = lax.axis_index("tm")
    steps = noisy.shape[1]
    barrier = pltpu.get_barrier_semaphore()
    for step in range(1, shots):
        pl.semaphore_signal(
            barrier, inc=1, device_id={"shot": lax.rem(me_shot + step, shots)}, device_id_type=MESH
        )
    for step in range(1, spans):
        pl.semaphore_signal(
            barrier, inc=1, device_id={"tm": lax.rem(me_tm + step, spans)}, device_id_type=MESH
        )
    pairs = [
        (cw, cw_v), (ow, ow_v), (lift, lift_v), (levw, levw_v), (gain, gain_v), (head, head_v),
        (level, level_v), (dil, dil_out), (missing, miss),
        (noisy, noisy_ext.at[:, pl.ds(HALO, steps), :]),
        (obs.at[pl.ds(2 * me_shot, 2)], landed.at[me_shot]),
    ]
    local = [pltpu.make_async_copy(a, b, local_sem.at[i]) for i, (a, b) in enumerate(pairs)]
    for copy in local:
        copy.start()
    pl.semaphore_wait(barrier, shots + spans - 2)

    right = {"tm": lax.rem(me_tm + 1, spans)}
    left = {"tm": lax.rem(me_tm + spans - 1, spans)}

    def halo(source, first, target, slot):
        up = pltpu.make_async_remote_copy(
            src_ref=source.at[:, pl.ds(first + steps - HALO, HALO), :],
            dst_ref=target.at[:, pl.ds(0, HALO), :],
            send_sem=halo_send.at[slot], recv_sem=halo_recv.at[slot],
            device_id=right, device_id_type=MESH,
        )
        down = pltpu.make_async_remote_copy(
            src_ref=source.at[:, pl.ds(first, HALO), :],
            dst_ref=target.at[:, pl.ds(HALO + steps, HALO), :],
            send_sem=halo_send.at[slot + 1], recv_sem=halo_recv.at[slot + 1],
            device_id=left, device_id_type=MESH,
        )
        up.start()
        down.start()
        return [up, down]

    exchange = []
    for step in range(1, shots):
        other = lax.rem(me_shot + step, shots)
        copy = pltpu.make_async_remote_copy(
            src_ref=obs.at[pl.ds(2 * other, 2)], dst_ref=landed.at[me_shot],
            send_sem=shot_send.at[step], recv_sem=shot_recv.at[step],
            device_id={"shot": other}, device_id_type=MESH,
        )
        copy.start()
        exchange.append(copy)
    halos = halo(noisy, 0, noisy_ext, 0)
    for copy in local:
        copy.wait()

    taps = cw.shape[1]
    for l in range(2):
        for k in range(0, taps, 2):
            count = min(2, taps - k)
            block = jnp.concatenate([cw_v[l, k + i] for i in range(count)], 0).astype(f32) * 0.5
            wt[l, :, k * 64 : (k + count) * 64] = block.T.astype(bf16)
    projection[...] = ow_v[0]
    folded = lax.dot_general(
        head_v[...], ow_v[1].astype(f32), (((1,), (0,)), ((), ())), precision=lax.Precision.HIGHEST
    )
    high = folded.astype(bf16)
    low = (folded - high.astype(f32)).astype(bf16)
    last[...] = jnp.concatenate([high, low, jnp.zeros((14, 256), bf16)], 0)
    cols[0] = column(lift_v[0:1, :])
    cols[1] = column(lift_v[1:2, :])
    cols[2] = column(gain_v[0:1, :])
    cols[3] = column(gain_v[1:2, :])
    cols[4] = column(head_v[...])
    present = (1 - miss[...]).astype(f32)
    for s in range(2):
        noise = jnp.broadcast_to(level_v[0:1, s : s + 1], (64, 128))
        shot_base[s] = column(lift_v[2:3, :]) * present[s : s + 1, :] + noise * column(levw_v[...])

    for copy in exchange:
        copy.wait_recv()
    masked = [landed[:, s].reshape(8 * shots, steps).T * present[s : s + 1, :] for s in range(2)]
    for s in range(2):
        sent[s : s + 1, :] = jnp.sum(masked[s] * masked[s], axis=0, keepdims=True)
    sharing = []
    for step in range(1, spans):
        other = lax.rem(me_tm + step, spans)
        copy = pltpu.make_async_remote_copy(
            src_ref=sent, dst_ref=sums.at[me_tm],
            send_sem=sum_send.at[step], recv_sem=sum_recv.at[step],
            device_id={"tm": other}, device_id_type=MESH,
        )
        copy.start()
        sharing.append(copy)
    for s in range(2):
        masked_ext[s, HALO : HALO + steps, :] = masked[s]
    halos += halo(masked_ext, HALO, masked_ext, 2)
    sums[me_tm] = sent[...]
    for copy in exchange:
        copy.wait_send()
    for copy in sharing:
        copy.wait_recv()
    total = jnp.sum(jnp.sum(sums[...], axis=0), axis=1, keepdims=True)
    total = jnp.broadcast_to(total, scale.shape)
    scale[...] = lax.rsqrt(total / (spans * steps * 8 * shots) + 1e-5)
    for copy in sharing:
        copy.wait_send()
    for copy in halos:
        copy.wait()


def exchange_inputs(shots, spans, *args):
    obs, noisy = args[:2]
    steps = noisy.shape[1]
    shape = jax.ShapeDtypeStruct
    ext = shape((2, steps + 2 * HALO, 8 * shots), f32)
    outs = (
        ext, ext, shape((2, 128), f32), shape((5, 64, 128), f32), shape((2, 64, 128), f32),
        shape((2, 256, 576), bf16), shape((64, 256), bf16), shape((16, 256), bf16),
        shape((1, 2), jnp.int32),
    )
    dma = pltpu.SemaphoreType.DMA
    return pl.pallas_call(
        lambda *refs: exchange_kernel(shots, spans, *refs),
        out_shape=outs,
        in_specs=[pl.BlockSpec(memory_space=pltpu.HBM)] * len(args),
        out_specs=(pl.BlockSpec(memory_space=pltpu.VMEM),) * len(outs),
        scratch_shapes=[
            pltpu.VMEM((shots, 2, 8, steps), f32),
            pltpu.VMEM((spans, 2, 128), f32),
            pltpu.VMEM((2, 128), f32),
        ] + [pltpu.VMEM(a.shape, a.dtype) for i, a in enumerate(args) if i in (2, 3, 5, 6, 7, 8, 9, 10)] + [
            dma((11,)), dma((shots,)), dma((shots,)), dma((4,)), dma((4,)), dma((spans,)), dma((spans,)),
        ],
        compiler_params=pltpu.CompilerParams(
            collective_id=0, has_side_effects=True, vmem_limit_bytes=24 * 2**20
        ),
        name="exchange",
    )(*args)


def gelu_of_half(h):
    u = h * (2 * TANH_SCALE + (8 * TANH_SCALE * TANH_CUBE) * (h * h))
    return (h + h * jnp.tanh(u)).astype(bf16)


def mm(a, b):
    return jnp.dot(a, b, preferred_element_type=f32)


def denoise_kernel(
    spans, masked, noisy, scale, cols, shot_base, wt, projection, last, dil, out, x1, x2, state, *sums
):
    steps = out.shape[1]
    total_time = spans * steps
    by = len(sums)
    d1, d2 = dil[0, 0], dil[0, 1]
    first = lax.axis_index("tm") * steps - HALO
    lane = lax.broadcasted_iota(jnp.int32, (64, 128), 1)
    zeros = jnp.zeros((64, 128), bf16)

    def put(ref, row, halves, d):
        halves = [a.astype(bf16) for a in halves]
        ref[row, 64:128, :] = jnp.concatenate(halves, 1)
        low = [jnp.where(lane >= d, pltpu.roll(a, d, 1), zeros) for a in halves]
        ref[row, 0:64, :] = jnp.concatenate(low, 1)
        high = [jnp.where(lane < 128 - d, pltpu.roll(a, 128 - d, 1), zeros) for a in halves]
        ref[row, 128:192, :] = jnp.concatenate(high, 1)

    def norm(a, g, row):
        time = row + first
        inside = jnp.where(jnp.logical_and(time >= 0, time < total_time), 1.0, 0.0).astype(f32)
        mean_square = jnp.sum(a * a, axis=0, keepdims=True) * (1.0 / 64)
        return a * (lax.rsqrt(mean_square + 1e-5) * inside) * g

    def lift_row(row):
        source = jnp.minimum(row, noisy.shape[1] - 1)
        normed = []
        for s in range(2):
            a = cols[0] * noisy[s, pl.ds(source, 1), :]
            a = a + cols[1] * (masked[s, pl.ds(source, 1), :] * scale[s : s + 1, :]) + shot_base[s]
            state[row, :, s * 128 : (s + 1) * 128] = a
            normed.append(norm(a, cols[2], row))
        put(x1, row, normed, d1)

    def conv(l, ref, r, d):
        return mm(wt[l], jnp.concatenate([ref[r - d], ref[r], ref[r + d]], 0))

    start = HALO - d2
    trips = (steps + 2 * d2 + by - 1) // by
    ahead = start - d1

    def lifts(q, carry):
        for u in range(by):
            lift_row(ahead + q * by + u)
        return carry

    before = (2 * d1 + by + by - 1) // by
    lax.fori_loop(0, before, lifts, 0)
    lifted = ahead + before * by
    for u in range(by):
        sums[u][...] = conv(0, x1, start + u, d1)
    for u in range(by):
        lift_row(lifted + u)
    lifted = lifted + by

    def first_end(r, act):
        updated = state[r] + mm(projection[...], act)
        state[r] = updated
        put(x2, r - DMAX, [norm(updated[:, s * 128 : (s + 1) * 128], cols[3], r) for s in range(2)], d2)

    def second_end(r, act):
        y = mm(last[...], act)
        y = y[0:1, :] + y[1:2, :]
        for s in range(2):
            lanes = slice(s * 128, (s + 1) * 128)
            h = jnp.sum(state[r + HALO, :, lanes] * cols[4], axis=0, keepdims=True)
            out[s, pl.ds(r, 1), :] = h + y[:, lanes]

    def first_block(q, carry):
        r = start + q * by
        for u in range(by):
            act = gelu_of_half(sums[u][...])
            sums[u][...] = conv(0, x1, r + by + u, d1)
            first_end(r + u, act)
        for u in range(by):
            lift_row(lifted + q * by + u)
        return carry

    lax.fori_loop(0, trips - 1, first_block, 0)
    r = start + (trips - 1) * by
    for u in range(by):
        act = gelu_of_half(sums[u][...])
        sums[u][...] = conv(1, x2, DMAX + u, d2)
        first_end(r + u, act)

    def second_block(q, carry):
        r = q * by
        for u in range(by):
            act = gelu_of_half(sums[u][...])
            sums[u][...] = conv(1, x2, DMAX + r + by + u, d2)
            second_end(r + u, act)
        return carry

    lax.fori_loop(0, steps // by - 1, second_block, 0)
    for u in range(by):
        second_end(steps - by + u, gelu_of_half(sums[u][...]))


def denoise(spans, *args):
    steps = args[0].shape[1] - 2 * HALO
    vm = pl.BlockSpec(memory_space=pltpu.VMEM)
    return pl.pallas_call(
        lambda *refs: denoise_kernel(spans, *refs),
        out_shape=jax.ShapeDtypeStruct((2, steps, 128), f32),
        in_specs=[vm] * len(args),
        out_specs=vm,
        scratch_shapes=[
            pltpu.VMEM((176, 192, 256), bf16),
            pltpu.VMEM((136, 192, 256), bf16),
            pltpu.VMEM((176, 64, 256), f32),
        ] + [pltpu.VMEM((256, 256), f32)] * UNROLL,
        compiler_params=pltpu.CompilerParams(vmem_limit_bytes=48 * 2**20),
        name="denoise",
    )(*args)


def solution(mesh):
    shots, spans = mesh.shape["shot"], mesh.shape["tm"]

    def per_device(
        noisy_gather, observed, missing, noise_level, dilations, lift_weight, level_weight,
        norm_gain, conv_weight, out_weight, head_weight,
    ):
        shared = exchange_inputs(
            shots, spans, jnp.swapaxes(observed, 1, 2), noisy_gather, missing, noise_level[None, :],
            dilations[None, :], lift_weight, level_weight[None, :], norm_gain, conv_weight,
            jnp.swapaxes(out_weight, 1, 2), head_weight[None, :],
        )
        return denoise(spans, *shared)

    return jax.shard_map(
        per_device,
        mesh=mesh,
        in_specs=(
            P("shot", "tm", None), P(None, "tm", "shot"), P("shot", None), P("shot"),
            P(), P(), P(), P(), P(), P(), P(),
        ),
        out_specs=P("shot", "tm", None),
        check_vma=False,
    )
```

time: 70.6 us -> 54.9 us (0.78)
  Pallas kernels: 66.1 us -> 50.2 us
    pallas_call x2, Pallas kernels: 66.1 us -> 50.2 us  [the longest x1 27.5 us: denoise(): pl.pallas_call(lambda *refs: denoise_kernel(spans, *refs), out_shape=jax....]
where the time goes in v2:
time: 54.9 us; the launch traced here: 54.6 us
  Pallas kernels  50.2 us (91%)
  local copies, waits for them, and re-layouts  4.37 us (8%)
    pallas_call x1, Pallas kernels, denoise(): pl.pallas_call(lambda *refs: denoise_kernel(spans, *refs), out_shape=jax....  27.5 us
    pallas_call x1, Pallas kernels, exchange_inputs(): pl.pallas_call(lambda *refs: exchange_kernel(shots, spans, *refs), out_sh...  22.7 us
    unnamed x22, local copies, waits for them, and re-layouts  4.37 us

profile of v2, /device:TPU:1, one launch (start us, length us, event | category | flops | bytes accessed | tf_op | source)
XLA Modules:
  0.0 54.6 jit_solution(851873395560889346)
XLA Ops:
  0.0 0.0 copy-start.10
  0.0 0.0 copy-start.6
  0.0 0.0 copy-start.8
  0.0 0.0 copy-start.9
  0.0 0.0 copy-start.4
  0.0 0.0 copy-start.5
  0.0 0.0 copy-start.7
  0.0 0.6 %copy-done.10 = f32[64]{0:T(128)S(1)} copy-done((f32[64]{0:T(128)S(1)}, f32[64]{0:T(128)}, u32[]{:S(2)}) %copy-start.10) | copy-done | bytes 280
  0.7 0.0 copy-done.6
  0.7 0.0 copy-done.8
  0.7 0.0 copy-done.9
  0.7 0.0 copy-done.4
  0.7 0.0 copy-done.5
  0.8 0.0 copy-done.7
  0.8 0.0 copy-start
  0.8 1.1 %copy-done = bf16[2,9,64,256]{3,2,1,0:T(8,128)(2,1)S(1)} copy-done((bf16[2,9,64,256]{3,2,1,0:T(8,128)(2,1)S(1)}, bf16[2,9,64,256]{3,2,1,0:T(8,128)(2,1)}, u32[]{:S(2)}) %copy-start) | copy-done | bytes 589848
  1.8 0.0 copy-start.1
  1.8 0.9 %copy-done.1 = f32[32,64,8]{1,2,0:T(8,128)S(1)} copy-done((f32[32,64,8]{1,2,0:T(8,128)S(1)}, f32[32,64,8]{1,2,0:T(8,128)}, u32[]{:S(2)}) %copy-start.1) | copy-done | bytes 65560
  2.7 0.0 copy-start.2
  2.7 0.8 %copy-done.2 = f32[2,64,128]{2,1,0:T(8,128)S(1)} copy-done((f32[2,64,128]{2,1,0:T(8,128)S(1)}, f32[2,64,128]{2,1,0:T(8,128)}, u32[]{:S(2)}) %copy-start.2) | copy-done | bytes 65560
  3.6 0.0 copy-start.3
  3.6 0.8 %copy-done.3 = bf16[2,256,64]{1,2,0:T(8,128)(2,1)S(1)} copy-done((bf16[2,256,64]{1,2,0:T(8,128)(2,1)S(1)}, bf16[2,256,64]{1,2,0:T(8,128)(2,1)}, u32[]{:S(2)}) %copy-start.3) | copy-done | bytes 65560
  4.4 22.7 %exchange.1 = (f32[2,128,128]{2,1,0:T(8,128)S(1)}, f32[2,128,128]{2,1,0:T(8,128)S(1)}, f32[2,128]{1,0:T(2,128)S(1)}, f32[5,64,128]{2,1,0:T(8,128)S(1)}, f32[2,64...) custom-call(f32[32,8,64]{2,1,0:T(8,128)S(1)} %bitcast.6, ...), custom_call_target="tpu_custom_call" | custom-call | tf_op jit(solution)/shard_map/exchange/pallas_call | solution.py:151
  27.1 27.5 %denoise.1 = f32[2,64,128]{2,1,0:T(8,128)} custom-call(f32[2,128,128]{2,1,0:T(8,128)S(1)} %get-tuple-element.14.refs_0_, f32[2,128,128]{2,1,0:T(8,128)S(1)} %get-tuple-element.15.refs_1_, f32[2,128]{1,0:T(2,128)S(1)} %get-tuple-element.16.refs_2_, f32[5,64,128]{2,1,0:T(8,128)S(1)} %get-tuple-element.17.refs_3_, f32[2,64,128]{2,1,0:T(8,128)S(1)} %get-tuple-element.18.refs_4_, ...), custom_call_target="tpu_custom_call" | custom-call | tf_op jit(solution)/shard_map/denoise/pallas_call | solution.py:281
Async XLA Ops:
  0.0 0.7 %copy-start.10 = (f32[64]{0:T(128)S(1)}, f32[64]{0:T(128)}, u32[]{:S(2)}) copy-start(f32[64]{0:T(128)} %param.21) | copy-start | bytes 772
  0.0 0.7 %copy-start.6 = (f32[2,64]{1,0:T(2,128)S(1)}, f32[2,64]{1,0:T(2,128)}, u32[]{:S(2)}) copy-start(f32[2,64]{1,0:T(2,128)} %refs_7_.1) | copy-start | bytes 1540
  0.0 0.7 %copy-start.8 = (s32[2]{0:T(128)S(1)}, s32[2]{0:T(128)}, u32[]{:S(2)}) copy-start(s32[2]{0:T(128)} %param.15) | copy-start | bytes 28
  0.0 0.7 %copy-start.9 = (f32[64]{0:T(128)S(1)}, f32[64]{0:T(128)}, u32[]{:S(2)}) copy-start(f32[64]{0:T(128)} %param.17) | copy-start | bytes 772
  0.0 0.7 %copy-start.4 = (f32[3,64]{1,0:T(4,128)S(1)}, f32[3,64]{1,0:T(4,128)}, u32[]{:S(2)}) copy-start(f32[3,64]{1,0:T(4,128)} %refs_5_.1) | copy-start | bytes 2308
  0.0 0.7 %copy-start.5 = (s32[2,128]{1,0:T(2,128)S(1)}, s32[2,128]{1,0:T(2,128)}, u32[]{:S(2)}) copy-start(s32[2,128]{1,0:T(2,128)} %refs_2_.1) | copy-start | bytes 3076
  0.0 0.7 %copy-start.7 = (f32[2]{0:T(128)S(1)}, f32[2]{0:T(128)}, u32[]{:S(2)}) copy-start(f32[2]{0:T(128)} %param.14) | copy-start | bytes 28
  0.8 1.1 %copy-start = (bf16[2,9,64,256]{3,2,1,0:T(8,128)(2,1)S(1)}, bf16[2,9,64,256]{3,2,1,0:T(8,128)(2,1)}, u32[]{:S(2)}) copy-start(bf16[2,9,64,256]{3,2,1,0:T(8,128)(2,1)} %refs_8_.1) | copy-start | bytes 1769476
  1.8 0.9 %copy-start.1 = (f32[32,64,8]{1,2,0:T(8,128)S(1)}, f32[32,64,8]{1,2,0:T(8,128)}, u32[]{:S(2)}) copy-start(f32[32,64,8]{1,2,0:T(8,128)} %param.12) | copy-start | bytes 196612
  2.7 0.8 %copy-start.2 = (f32[2,64,128]{2,1,0:T(8,128)S(1)}, f32[2,64,128]{2,1,0:T(8,128)}, u32[]{:S(2)}) copy-start(f32[2,64,128]{2,1,0:T(8,128)} %refs_1_.1) | copy-start | bytes 196612
  3.6 0.8 %copy-start.3 = (bf16[2,256,64]{1,2,0:T(8,128)(2,1)S(1)}, bf16[2,256,64]{1,2,0:T(8,128)(2,1)}, u32[]{:S(2)}) copy-start(bf16[2,256,64]{1,2,0:T(8,128)(2,1)} %param.20) | copy-start | bytes 196612

commit v3 on v2

--- a/solution.py
+++ b/solution.py
@@ -20,10 +20,10 @@
 
 def exchange_kernel(
     shots, spans,
-    obs, noisy, missing, level, dil, lift, levw, gain, cw, ow, head,
-    masked_ext, noisy_ext, scale, cols, shot_base, wt, projection, last, dil_out,
-    landed, sums, sent, miss, level_v, lift_v, levw_v, gain_v, cw_v, ow_v, head_v,
-    local_sem, shot_send, shot_recv, halo_send, halo_recv, sum_send, sum_recv,
+    obs, noisy, missing, level, lift, levw, gain, cw, ow, head,
+    masked_ext, noisy_ext, sums, cols_out, shot_base_out, wt_out, last_out,
+    landed, sent, masked, cols, shot_base, wt, last, miss, level_v, lift_v, levw_v, gain_v, cw_v, ow_v, head_v,
+    local_sem, out_sem, shot_send, shot_recv, halo_send, halo_recv, sum_send, sum_recv,
 ):
     me_shot = lax.axis_index("shot")
     me_tm = lax.axis_index("tm")
@@ -39,7 +39,7 @@
         )
     pairs = [
         (cw, cw_v), (ow, ow_v), (lift, lift_v), (levw, levw_v), (gain, gain_v), (head, head_v),
-        (level, level_v), (dil, dil_out), (missing, miss),
+        (level, level_v), (missing, miss),
         (noisy, noisy_ext.at[:, pl.ds(HALO, steps), :]),
         (obs.at[pl.ds(2 * me_shot, 2)], landed.at[me_shot]),
     ]
@@ -88,7 +88,6 @@
             count = min(2, taps - k)
             block = jnp.concatenate([cw_v[l, k + i] for i in range(count)], 0).astype(f32) * 0.5
             wt[l, :, k * 64 : (k + count) * 64] = block.T.astype(bf16)
-    projection[...] = ow_v[0]
     folded = lax.dot_general(
         head_v[...], ow_v[1].astype(f32), (((1,), (0,)), ((), ())), precision=lax.Precision.HIGHEST
     )
@@ -105,11 +104,19 @@
         noise = jnp.broadcast_to(level_v[0:1, s : s + 1], (64, 128))
         shot_base[s] = column(lift_v[2:3, :]) * present[s : s + 1, :] + noise * column(levw_v[...])
 
+    results = [
+        pltpu.make_async_copy(a, b, out_sem.at[i])
+        for i, (a, b) in enumerate([(cols, cols_out), (shot_base, shot_base_out), (wt, wt_out), (last, last_out)])
+    ]
+    for copy in results:
+        copy.start()
+
     for copy in exchange:
         copy.wait_recv()
-    masked = [landed[:, s].reshape(8 * shots, steps).T * present[s : s + 1, :] for s in range(2)]
     for s in range(2):
-        sent[s : s + 1, :] = jnp.sum(masked[s] * masked[s], axis=0, keepdims=True)
+        rows = landed[:, s].reshape(8 * shots, steps).T * present[s : s + 1, :]
+        masked[s] = rows
+        sent[s : s + 1, :] = jnp.sum(rows * rows, axis=0, keepdims=True)
     sharing = []
     for step in range(1, spans):
         other = lax.rem(me_tm + step, spans)
@@ -120,20 +127,18 @@
         )
         copy.start()
         sharing.append(copy)
-    for s in range(2):
-        masked_ext[s, HALO : HALO + steps, :] = masked[s]
-    halos += halo(masked_ext, HALO, masked_ext, 2)
-    sums[me_tm] = sent[...]
+    halos += halo(masked, 0, masked_ext, 2)
+    mine = [
+        pltpu.make_async_copy(sent, sums.at[me_tm], out_sem.at[4]),
+        pltpu.make_async_copy(masked, masked_ext.at[:, pl.ds(HALO, steps), :], out_sem.at[5]),
+    ]
+    for copy in mine:
+        copy.start()
     for copy in exchange:
         copy.wait_send()
-    for copy in sharing:
-        copy.wait_recv()
-    total = jnp.sum(jnp.sum(sums[...], axis=0), axis=1, keepdims=True)
-    total = jnp.broadcast_to(total, scale.shape)
-    scale[...] = lax.rsqrt(total / (spans * steps * 8 * shots) + 1e-5)
-    for copy in sharing:
-        copy.wait_send()
-    for copy in halos:
+    for copy in results + mine:
+        copy.wait()
+    for copy in sharing + halos:
         copy.wait()
 
 
@@ -142,26 +147,28 @@
     steps = noisy.shape[1]
     shape = jax.ShapeDtypeStruct
     ext = shape((2, steps + 2 * HALO, 8 * shots), f32)
-    outs = (
-        ext, ext, shape((2, 128), f32), shape((5, 64, 128), f32), shape((2, 64, 128), f32),
-        shape((2, 256, 576), bf16), shape((64, 256), bf16), shape((16, 256), bf16),
-        shape((1, 2), jnp.int32),
+    built = (
+        shape((5, 64, 128), f32), shape((2, 64, 128), f32), shape((2, 256, 576), bf16),
+        shape((16, 256), bf16),
     )
+    outs = (ext, ext, shape((spans, 2, 128), f32)) + built
     dma = pltpu.SemaphoreType.DMA
+    staged = [args[i] for i in (2, 3, 4, 5, 6, 7, 8, 9)]
+    hbm = pl.BlockSpec(memory_space=pltpu.HBM)
     return pl.pallas_call(
         lambda *refs: exchange_kernel(shots, spans, *refs),
         out_shape=outs,
-        in_specs=[pl.BlockSpec(memory_space=pltpu.HBM)] * len(args),
-        out_specs=(pl.BlockSpec(memory_space=pltpu.VMEM),) * len(outs),
+        in_specs=[hbm] * len(args),
+        out_specs=(hbm,) * len(outs),
         scratch_shapes=[
             pltpu.VMEM((shots, 2, 8, steps), f32),
-            pltpu.VMEM((spans, 2, 128), f32),
             pltpu.VMEM((2, 128), f32),
-        ] + [pltpu.VMEM(a.shape, a.dtype) for i, a in enumerate(args) if i in (2, 3, 5, 6, 7, 8, 9, 10)] + [
-            dma((11,)), dma((shots,)), dma((shots,)), dma((4,)), dma((4,)), dma((spans,)), dma((spans,)),
+            pltpu.VMEM((2, steps, 128), f32),
+        ] + [pltpu.VMEM(a.shape, a.dtype) for a in built] + [pltpu.VMEM(a.shape, a.dtype) for a in staged] + [
+            dma((10,)), dma((6,)), dma((shots,)), dma((shots,)), dma((4,)), dma((4,)), dma((spans,)), dma((spans,)),
         ],
         compiler_params=pltpu.CompilerParams(
-            collective_id=0, has_side_effects=True, vmem_limit_bytes=24 * 2**20
+            collective_id=0, has_side_effects=True, vmem_limit_bytes=58 * 2**20
         ),
         name="exchange",
     )(*args)
@@ -177,12 +184,25 @@
 
 
 def denoise_kernel(
-    spans, masked, noisy, scale, cols, shot_base, wt, projection, last, dil, out, x1, x2, state, *sums
+    spans,
+    dil_in, noisy_in, masked_in, shares_in, cols_in, shot_base_in, wt_in, ow_in, last_in, out,
+    dil, noisy, masked, shares, cols, shot_base, wt, ow, last, sem, x1, x2, state, *sums
 ):
     steps = out.shape[1]
     total_time = spans * steps
     by = len(sums)
-    d1, d2 = dil[0, 0], dil[0, 1]
+    pairs = [
+        (dil_in, dil), (noisy_in, noisy), (masked_in, masked), (shares_in, shares), (cols_in, cols),
+        (shot_base_in, shot_base), (wt_in, wt), (ow_in, ow), (last_in, last),
+    ]
+    loads = [pltpu.make_async_copy(a, b, sem.at[i]) for i, (a, b) in enumerate(pairs)]
+    for copy in loads:
+        copy.start()
+    for copy in loads[:6]:
+        copy.wait()
+    d1, d2 = dil[0], dil[1]
+    energy = jnp.sum(jnp.sum(shares[...], axis=0), axis=1, keepdims=True)
+    scale = lax.rsqrt(jnp.broadcast_to(energy, (2, 128)) / (total_time * 128) + 1e-5)
     first = lax.axis_index("tm") * steps - HALO
     lane = lax.broadcasted_iota(jnp.int32, (64, 128), 1)
     zeros = jnp.zeros((64, 128), bf16)
@@ -206,7 +226,7 @@
         normed = []
         for s in range(2):
             a = cols[0] * noisy[s, pl.ds(source, 1), :]
-            a = a + cols[1] * (masked[s, pl.ds(source, 1), :] * scale[s : s + 1, :]) + shot_base[s]
+            a = a + cols[1] * (masked[s, pl.ds(source, 1), :] * scale[s : s + 1]) + shot_base[s]
             state[row, :, s * 128 : (s + 1) * 128] = a
             normed.append(norm(a, cols[2], row))
         put(x1, row, normed, d1)
@@ -226,6 +246,8 @@
     before = (2 * d1 + by + by - 1) // by
     lax.fori_loop(0, before, lifts, 0)
     lifted = ahead + before * by
+    for copy in loads[6:]:
+        copy.wait()
     for u in range(by):
         sums[u][...] = conv(0, x1, start + u, d1)
     for u in range(by):
@@ -233,7 +255,7 @@
     lifted = lifted + by
 
     def first_end(r, act):
-        updated = state[r] + mm(projection[...], act)
+        updated = state[r] + mm(ow[0], act)
         state[r] = updated
         put(x2, r - DMAX, [norm(updated[:, s * 128 : (s + 1) * 128], cols[3], r) for s in range(2)], d2)
 
@@ -275,22 +297,23 @@
         second_end(steps - by + u, gelu_of_half(sums[u][...]))
 
 
-def denoise(spans, *args):
+def denoise(spans, dil, *args):
     steps = args[0].shape[1] - 2 * HALO
-    vm = pl.BlockSpec(memory_space=pltpu.VMEM)
+    hbm = pl.BlockSpec(memory_space=pltpu.HBM)
     return pl.pallas_call(
         lambda *refs: denoise_kernel(spans, *refs),
         out_shape=jax.ShapeDtypeStruct((2, steps, 128), f32),
-        in_specs=[vm] * len(args),
-        out_specs=vm,
-        scratch_shapes=[
+        in_specs=[hbm] * (1 + len(args)),
+        out_specs=pl.BlockSpec(memory_space=pltpu.VMEM),
+        scratch_shapes=[pltpu.SMEM((2,), jnp.int32)] + [pltpu.VMEM(a.shape, a.dtype) for a in args] + [
+            pltpu.SemaphoreType.DMA((9,)),
             pltpu.VMEM((176, 192, 256), bf16),
             pltpu.VMEM((136, 192, 256), bf16),
             pltpu.VMEM((176, 64, 256), f32),
         ] + [pltpu.VMEM((256, 256), f32)] * UNROLL,
-        compiler_params=pltpu.CompilerParams(vmem_limit_bytes=48 * 2**20),
+        compiler_params=pltpu.CompilerParams(vmem_limit_bytes=58 * 2**20),
         name="denoise",
-    )(*args)
+    )(dil, *args)
 
 
 def solution(mesh):
@@ -300,12 +323,12 @@
         noisy_gather, observed, missing, noise_level, dilations, lift_weight, level_weight,
         norm_gain, conv_weight, out_weight, head_weight,
     ):
-        shared = exchange_inputs(
+        projections = jnp.swapaxes(out_weight, 1, 2)
+        masked, noisy, shares, cols, shot_base, wt, last = exchange_inputs(
             shots, spans, jnp.swapaxes(observed, 1, 2), noisy_gather, missing, noise_level[None, :],
-            dilations[None, :], lift_weight, level_weight[None, :], norm_gain, conv_weight,
-            jnp.swapaxes(out_weight, 1, 2), head_weight[None, :],
-        )
-        return denoise(spans, *shared)
+            lift_weight, level_weight[None, :], norm_gain, conv_weight, projections, head_weight[None, :],
+        )
+        return denoise(spans, dilations, noisy, masked, shares, cols, shot_base, wt, projections, last)
 
     return jax.shard_map(
         per_device,

time: 54.9 us -> 55.5 us (1.011)
  Pallas kernels: 50.2 us -> 55.4 us
  local copies, waits for them, and re-layouts: 4.37 us -> 0 us
    pallas_call x1, Pallas kernels: 27.5 us -> 32.5 us  [denoise(): pl.pallas_call(lambda *refs: denoise_kernel(spans, *refs), out_shape=jax....]
    unnamed x22 -> x0, local copies, waits for them, and re-layouts: 4.37 us -> none
where the time goes in v3:
time: 55.5 us; the launch traced here: 55.4 us
  Pallas kernels  55.4 us (100%)
    pallas_call x1, Pallas kernels, denoise(): pl.pallas_call(lambda *refs: denoise_kernel(spans, *refs), out_shape=jax....  32.5 us
    pallas_call x1, Pallas kernels, exchange_inputs(): pl.pallas_call(lambda *refs: exchange_kernel(shots, spans, *refs), out_sh...  22.9 us

profile of v3, /device:TPU:1, one launch (start us, length us, event | category | flops | bytes accessed | tf_op | source)
XLA Modules:
  0.0 55.4 jit_solution(16278103595954891844)
XLA Ops:
  0.0 22.9 %exchange.1 = (f32[2,128,128]{2,1,0:T(8,128)}, f32[2,128,128]{2,1,0:T(8,128)}, f32[16,2,128]{2,1,0:T(2,128)}, f32[5,64,128]{2,1,0:T(8,128)}, f32[2,64,128]{2,1,0...) custom-call(f32[32,8,64]{2,1,0:T(8,128)} %bitcast.7, f32[2,64,128]{2,1,0:T(8,128)} %refs_1_.1, ...), custom_call_target="tpu_custom_call" | custom-call | tf_op jit(solution)/shard_map/exchange/pallas_call | solution.py:158
  22.9 32.5 %denoise.1 = f32[2,64,128]{2,1,0:T(8,128)} custom-call(s32[2]{0:T(128)} %refs_0_.1, f32[2,128,128]{2,1,0:T(8,128)} %get-tuple-element.12.refs_1_, f32[2,128,128]{2,1,0:T(8,128)} %get-tuple-element.13.refs_2_, f32[16,2,128]{2,1,0:T(2,128)} %get-tuple-element.14.refs_3_, f32[5,64,128]{2,1,0:T(8,128)} %get-tuple-element.15.refs_4_, ...), custom_call_target="tpu_custom_call" | custom-call | tf_op jit(solution)/shard_map/denoise/pallas_call | solution.py:303

commit v4 on v3

--- a/solution.py
+++ b/solution.py
@@ -10,7 +10,7 @@
 HALO = 2 * DMAX
 TANH_SCALE = 0.7978845608028654
 TANH_CUBE = 0.044715
-UNROLL = 8
+EARLY, JOINT, RING = 8, 12, 4
 f32, bf16 = jnp.float32, jnp.bfloat16
 
 
@@ -186,11 +186,11 @@
 def denoise_kernel(
     spans,
     dil_in, noisy_in, masked_in, shares_in, cols_in, shot_base_in, wt_in, ow_in, last_in, out,
-    dil, noisy, masked, shares, cols, shot_base, wt, ow, last, sem, x1, x2, state, *sums
+    dil, noisy, masked, shares, cols, shot_base, wt, ow, last, sem, x1, x2, state, heads, *sums
 ):
     steps = out.shape[1]
     total_time = spans * steps
-    by = len(sums)
+    sums1, sums2 = sums[:RING], sums[RING:]
     pairs = [
         (dil_in, dil), (noisy_in, noisy), (masked_in, masked), (shares_in, shares), (cols_in, cols),
         (shot_base_in, shot_base), (wt_in, wt), (ow_in, ow), (last_in, last),
@@ -234,67 +234,70 @@
     def conv(l, ref, r, d):
         return mm(wt[l], jnp.concatenate([ref[r - d], ref[r], ref[r + d]], 0))
 
-    start = HALO - d2
-    trips = (steps + 2 * d2 + by - 1) // by
+    lead = RING + JOINT + d2
+    early = (lead + d2 + EARLY - 1) // EARLY
+    start = HALO + lead - early * EARLY
     ahead = start - d1
 
     def lifts(q, carry):
-        for u in range(by):
-            lift_row(ahead + q * by + u)
+        for u in range(8):
+            lift_row(ahead + q * 8 + u)
         return carry
 
-    before = (2 * d1 + by + by - 1) // by
+    before = (2 * d1 + RING + JOINT + 7) // 8
     lax.fori_loop(0, before, lifts, 0)
-    lifted = ahead + before * by
+    lifted = ahead + before * 8
     for copy in loads[6:]:
         copy.wait()
-    for u in range(by):
-        sums[u][...] = conv(0, x1, start + u, d1)
-    for u in range(by):
-        lift_row(lifted + u)
-    lifted = lifted + by
+    for u in range(RING):
+        sums1[u][...] = conv(0, x1, start + u, d1)
 
     def first_end(r, act):
         updated = state[r] + mm(ow[0], act)
-        state[r] = updated
-        put(x2, r - DMAX, [norm(updated[:, s * 128 : (s + 1) * 128], cols[3], r) for s in range(2)], d2)
+        halves = [updated[:, s * 128 : (s + 1) * 128] for s in range(2)]
+        heads[r] = jnp.concatenate([jnp.sum(a * cols[4], axis=0, keepdims=True) for a in halves], 1)
+        put(x2, r - DMAX, [norm(a, cols[3], r) for a in halves], d2)
 
     def second_end(r, act):
         y = mm(last[...], act)
-        y = y[0:1, :] + y[1:2, :]
+        y = y[0:1, :] + y[1:2, :] + heads[r + HALO]
         for s in range(2):
-            lanes = slice(s * 128, (s + 1) * 128)
-            h = jnp.sum(state[r + HALO, :, lanes] * cols[4], axis=0, keepdims=True)
-            out[s, pl.ds(r, 1), :] = h + y[:, lanes]
-
-    def first_block(q, carry):
-        r = start + q * by
-        for u in range(by):
-            act = gelu_of_half(sums[u][...])
-            sums[u][...] = conv(0, x1, r + by + u, d1)
+            out[s, pl.ds(r, 1), :] = y[:, s * 128 : (s + 1) * 128]
+
+    def first_block(r, count):
+        for u in range(count):
+            act = gelu_of_half(sums1[u % RING][...])
+            sums1[u % RING][...] = conv(0, x1, r + RING + u, d1)
             first_end(r + u, act)
-        for u in range(by):
-            lift_row(lifted + q * by + u)
+
+    def second_block(r, count, lift_from=None):
+        for u in range(count):
+            act = gelu_of_half(sums2[u % RING][...])
+            sums2[u % RING][...] = conv(1, x2, DMAX + r + RING + u, d2)
+            second_end(r + u, act)
+            if lift_from is not None:
+                lift_row(lift_from + u)
+
+    def alone(q, carry):
+        first_block(start + q * EARLY, EARLY)
+        for u in range(EARLY):
+            lift_row(lifted + q * EARLY + u)
         return carry
 
-    lax.fori_loop(0, trips - 1, first_block, 0)
-    r = start + (trips - 1) * by
-    for u in range(by):
-        act = gelu_of_half(sums[u][...])
-        sums[u][...] = conv(1, x2, DMAX + u, d2)
-        first_end(r + u, act)
-
-    def second_block(q, carry):
-        r = q * by
-        for u in range(by):
-            act = gelu_of_half(sums[u][...])
-            sums[u][...] = conv(1, x2, DMAX + r + by + u, d2)
-            second_end(r + u, act)
+    lax.fori_loop(0, early, alone, 0)
+    for u in range(RING):
+        sums2[u][...] = conv(1, x2, DMAX + u, d2)
+
+    def joint(q, carry):
+        second_block(q * JOINT, JOINT, lifted + early * EARLY + q * JOINT)
+        first_block(HALO + lead + q * JOINT, JOINT)
         return carry
 
-    lax.fori_loop(0, steps // by - 1, second_block, 0)
-    for u in range(by):
-        second_end(steps - by + u, gelu_of_half(sums[u][...]))
+    trips = (steps - RING - JOINT) // JOINT
+    lax.fori_loop(0, trips, joint, 0)
+    second_block(trips * JOINT, JOINT)
+    for u in range(RING):
+        second_end(steps - RING + u, gelu_of_half(sums2[u][...]))
 
 
 def denoise(spans, dil, *args):
@@ -307,10 +310,11 @@
         out_specs=pl.BlockSpec(memory_space=pltpu.VMEM),
         scratch_shapes=[pltpu.SMEM((2,), jnp.int32)] + [pltpu.VMEM(a.shape, a.dtype) for a in args] + [
             pltpu.SemaphoreType.DMA((9,)),
-            pltpu.VMEM((176, 192, 256), bf16),
-            pltpu.VMEM((136, 192, 256), bf16),
-            pltpu.VMEM((176, 64, 256), f32),
-        ] + [pltpu.VMEM((256, 256), f32)] * UNROLL,
+            pltpu.VMEM((160, 192, 256), bf16),
+            pltpu.VMEM((112, 192, 256), bf16),
+            pltpu.VMEM((160, 64, 256), f32),
+            pltpu.VMEM((128, 1, 256), f32),
+        ] + [pltpu.VMEM((256, 256), f32)] * (2 * RING),
         compiler_params=pltpu.CompilerParams(vmem_limit_bytes=58 * 2**20),
         name="denoise",
     )(dil, *args)

time: 55.5 us -> 53.7 us (0.968)
  Pallas kernels: 55.4 us -> 53.6 us
    pallas_call x1, Pallas kernels: 32.5 us -> 30.7 us  [denoise(): pl.pallas_call(lambda *refs: denoise_kernel(spans, *refs), out_shape=jax....]
where the time goes in v4:
time: 53.7 us
  Pallas kernels  53.6 us (100%)
    pallas_call x1, Pallas kernels, denoise(): pl.pallas_call(lambda *refs: denoise_kernel(spans, *refs), out_shape=jax....  30.7 us
    pallas_call x1, Pallas kernels, exchange_inputs(): pl.pallas_call(lambda *refs: exchange_kernel(shots, spans, *refs), out_sh...  22.9 us

profile of v4, /device:TPU:1, one launch (start us, length us, event | category | flops | bytes accessed | tf_op | source)
XLA Modules:
  0.0 53.7 jit_solution(1092726011331904775)
XLA Ops:
  0.0 22.9 %exchange.1 = (f32[2,128,128]{2,1,0:T(8,128)}, f32[2,128,128]{2,1,0:T(8,128)}, f32[16,2,128]{2,1,0:T(2,128)}, f32[5,64,128]{2,1,0:T(8,128)}, f32[2,64,128]{2,1,0...) custom-call(f32[32,8,64]{2,1,0:T(8,128)} %bitcast.7, f32[2,64,128]{2,1,0:T(8,128)} %refs_1_.1, ...), custom_call_target="tpu_custom_call" | custom-call | tf_op jit(solution)/shard_map/exchange/pallas_call | solution.py:158
  22.9 30.7 %denoise.1 = f32[2,64,128]{2,1,0:T(8,128)} custom-call(s32[2]{0:T(128)} %refs_0_.1, f32[2,128,128]{2,1,0:T(8,128)} %get-tuple-element.12.refs_1_, f32[2,128,128]{2,1,0:T(8,128)} %get-tuple-element.13.refs_2_, f32[16,2,128]{2,1,0:T(2,128)} %get-tuple-element.14.refs_3_, f32[5,64,128]{2,1,0:T(8,128)} %get-tuple-element.15.refs_4_, ...), custom_call_target="tpu_custom_call" | custom-call | tf_op jit(solution)/shard_map/denoise/pallas_call | solution.py:306

commit v5 on v4

--- a/solution.py
+++ b/solution.py
@@ -10,7 +10,7 @@
 HALO = 2 * DMAX
 TANH_SCALE = 0.7978845608028654
 TANH_CUBE = 0.044715
-EARLY, JOINT, RING = 8, 12, 4
+EARLY, JOINT, RING, LIFTS = 12, 12, 4, 9
 f32, bf16 = jnp.float32, jnp.bfloat16
 
 
@@ -22,7 +22,7 @@
     shots, spans,
     obs, noisy, missing, level, lift, levw, gain, cw, ow, head,
     masked_ext, noisy_ext, sums, cols_out, shot_base_out, wt_out, last_out,
-    landed, sent, masked, cols, shot_base, wt, last, miss, level_v, lift_v, levw_v, gain_v, cw_v, ow_v, head_v,
+    landed, obs_v, packed, sent, masked, cols, shot_base, wt, last, miss, level_v, lift_v, levw_v, gain_v, cw_v, ow_v, head_v,
     local_sem, out_sem, shot_send, shot_recv, halo_send, halo_recv, sum_send, sum_recv,
 ):
     me_shot = lax.axis_index("shot")
@@ -41,11 +41,15 @@
         (cw, cw_v), (ow, ow_v), (lift, lift_v), (levw, levw_v), (gain, gain_v), (head, head_v),
         (level, level_v), (missing, miss),
         (noisy, noisy_ext.at[:, pl.ds(HALO, steps), :]),
-        (obs.at[pl.ds(2 * me_shot, 2)], landed.at[me_shot]),
+        (obs, obs_v),
     ]
     local = [pltpu.make_async_copy(a, b, local_sem.at[i]) for i, (a, b) in enumerate(pairs)]
     for copy in local:
         copy.start()
+    local.pop().wait()
+    for k in range(shots):
+        packed[k] = jnp.concatenate([obs_v[2 * k], obs_v[2 * k + 1]], 1)
+    landed[me_shot] = packed[me_shot]
     pl.semaphore_wait(barrier, shots + spans - 2)
 
     right = {"tm": lax.rem(me_tm + 1, spans)}
@@ -72,7 +76,7 @@
     for step in range(1, shots):
         other = lax.rem(me_shot + step, shots)
         copy = pltpu.make_async_remote_copy(
-            src_ref=obs.at[pl.ds(2 * other, 2)], dst_ref=landed.at[me_shot],
+            src_ref=packed.at[other], dst_ref=landed.at[me_shot],
             send_sem=shot_send.at[step], recv_sem=shot_recv.at[step],
             device_id={"shot": other}, device_id_type=MESH,
         )
@@ -113,8 +117,9 @@
 
     for copy in exchange:
         copy.wait_recv()
+    arrived = landed[...].reshape(8 * shots, 2 * steps).T
     for s in range(2):
-        rows = landed[:, s].reshape(8 * shots, steps).T * present[s : s + 1, :]
+        rows = arrived[s * steps : (s + 1) * steps] * present[s : s + 1, :]
         masked[s] = rows
         sent[s : s + 1, :] = jnp.sum(rows * rows, axis=0, keepdims=True)
     sharing = []
@@ -161,7 +166,9 @@
         in_specs=[hbm] * len(args),
         out_specs=(hbm,) * len(outs),
         scratch_shapes=[
-            pltpu.VMEM((shots, 2, 8, steps), f32),
+            pltpu.VMEM((shots, 8, 2 * steps), f32),
+            pltpu.VMEM(obs.shape, f32),
+            pltpu.VMEM((shots, 8, 2 * steps), f32),
             pltpu.VMEM((2, 128), f32),
             pltpu.VMEM((2, steps, 128), f32),
         ] + [pltpu.VMEM(a.shape, a.dtype) for a in built] + [pltpu.VMEM(a.shape, a.dtype) for a in staged] + [
@@ -275,7 +282,7 @@
             act = gelu_of_half(sums2[u % RING][...])
             sums2[u % RING][...] = conv(1, x2, DMAX + r + RING + u, d2)
             second_end(r + u, act)
-            if lift_from is not None:
+            if lift_from is not None and u < LIFTS:
                 lift_row(lift_from + u)
 
     def alone(q, carry):
@@ -289,7 +296,7 @@
         sums2[u][...] = conv(1, x2, DMAX + u, d2)
 
     def joint(q, carry):
-        second_block(q * JOINT, JOINT, lifted + early * EARLY + q * JOINT)
+        second_block(q * JOINT, JOINT, lifted + early * EARLY + q * LIFTS)
         first_block(HALO + lead + q * JOINT, JOINT)
         return carry
 

time: 53.7 us -> 52.2 us (0.972)
  Pallas kernels: 53.6 us -> 52.1 us
    pallas_call x1, Pallas kernels: 30.7 us -> 29.8 us  [denoise(): pl.pallas_call(lambda *refs: denoise_kernel(spans, *refs), out_shape=jax....]
    pallas_call x1, Pallas kernels: 22.9 us -> 22.2 us  [exchange_inputs(): pl.pallas_call(lambda *refs: exchange_kernel(shots, spans, *refs), out_sh...]
where the time goes in v5:
time: 52.2 us; the launch traced here: 52.1 us
  Pallas kernels  52.1 us (100%)
    pallas_call x1, Pallas kernels, denoise(): pl.pallas_call(lambda *refs: denoise_kernel(spans, *refs), out_shape=jax....  29.8 us
    pallas_call x1, Pallas kernels, exchange_inputs(): pl.pallas_call(lambda *refs: exchange_kernel(shots, spans, *refs), out_sh...  22.2 us

profile of v5, /device:TPU:1, one launch (start us, length us, event | category | flops | bytes accessed | tf_op | source)
XLA Modules:
  0.0 52.1 jit_solution(14015375059129810764)
XLA Ops:
  0.0 22.2 %exchange.1 = (f32[2,128,128]{2,1,0:T(8,128)}, f32[2,128,128]{2,1,0:T(8,128)}, f32[16,2,128]{2,1,0:T(2,128)}, f32[5,64,128]{2,1,0:T(8,128)}, f32[2,64,128]{2,1,0...) custom-call(f32[32,8,64]{2,1,0:T(8,128)} %bitcast.7, f32[2,64,128]{2,1,0:T(8,128)} %refs_1_.1, ...), custom_call_target="tpu_custom_call" | custom-call | tf_op jit(solution)/shard_map/exchange/pallas_call | solution.py:163
  22.2 29.8 %denoise.1 = f32[2,64,128]{2,1,0:T(8,128)} custom-call(s32[2]{0:T(128)} %refs_0_.1, f32[2,128,128]{2,1,0:T(8,128)} %get-tuple-element.12.refs_1_, f32[2,128,128]{2,1,0:T(8,128)} %get-tuple-element.13.refs_2_, f32[16,2,128]{2,1,0:T(2,128)} %get-tuple-element.14.refs_3_, f32[5,64,128]{2,1,0:T(8,128)} %get-tuple-element.15.refs_4_, ...), custom_call_target="tpu_custom_call" | custom-call | tf_op jit(solution)/shard_map/denoise/pallas_call | solution.py:313

commit v6 on v5

--- a/solution.py
+++ b/solution.py
@@ -21,8 +21,8 @@
 def exchange_kernel(
     shots, spans,
     obs, noisy, missing, level, lift, levw, gain, cw, ow, head,
-    masked_ext, noisy_ext, sums, cols_out, shot_base_out, wt_out, last_out,
-    landed, obs_v, packed, sent, masked, cols, shot_base, wt, last, miss, level_v, lift_v, levw_v, gain_v, cw_v, ow_v, head_v,
+    masked_ext, noisy_ext, sums, cols_out, shot_base_out, wt_out, proj_out, last_out,
+    landed, obs_v, packed, sent, masked, cols, shot_base, wt, proj, last, miss, level_v, lift_v, levw_v, gain_v, cw_v, ow_v, head_v,
     local_sem, out_sem, shot_send, shot_recv, halo_send, halo_recv, sum_send, sum_recv,
 ):
     me_shot = lax.axis_index("shot")
@@ -92,12 +92,14 @@
             count = min(2, taps - k)
             block = jnp.concatenate([cw_v[l, k + i] for i in range(count)], 0).astype(f32) * 0.5
             wt[l, :, k * 64 : (k + count) * 64] = block.T.astype(bf16)
-    folded = lax.dot_general(
-        head_v[...], ow_v[1].astype(f32), (((1,), (0,)), ((), ())), precision=lax.Precision.HIGHEST
-    )
-    high = folded.astype(bf16)
-    low = (folded - high.astype(f32)).astype(bf16)
-    last[...] = jnp.concatenate([high, low, jnp.zeros((14, 256), bf16)], 0)
+    for l, (ref, ahead) in enumerate([(proj, ow_v[0]), (last, None)]):
+        folded = lax.dot_general(
+            head_v[...], ow_v[l].astype(f32), (((1,), (0,)), ((), ())), precision=lax.Precision.HIGHEST
+        )
+        high = folded.astype(bf16)
+        low = (folded - high.astype(f32)).astype(bf16)
+        rows = [high, low, jnp.zeros((14, 256), bf16)]
+        ref[...] = jnp.concatenate(rows if ahead is None else [ahead] + rows, 0)
     cols[0] = column(lift_v[0:1, :])
     cols[1] = column(lift_v[1:2, :])
     cols[2] = column(gain_v[0:1, :])
@@ -110,7 +112,7 @@
 
     results = [
         pltpu.make_async_copy(a, b, out_sem.at[i])
-        for i, (a, b) in enumerate([(cols, cols_out), (shot_base, shot_base_out), (wt, wt_out), (last, last_out)])
+        for i, (a, b) in enumerate([(cols, cols_out), (shot_base, shot_base_out), (wt, wt_out), (proj, proj_out), (last, last_out)])
     ]
     for copy in results:
         copy.start()
@@ -134,8 +136,8 @@
         sharing.append(copy)
     halos += halo(masked, 0, masked_ext, 2)
     mine = [
-        pltpu.make_async_copy(sent, sums.at[me_tm], out_sem.at[4]),
-        pltpu.make_async_copy(masked, masked_ext.at[:, pl.ds(HALO, steps), :], out_sem.at[5]),
+        pltpu.make_async_copy(sent, sums.at[me_tm], out_sem.at[5]),
+        pltpu.make_async_copy(masked, masked_ext.at[:, pl.ds(HALO, steps), :], out_sem.at[6]),
     ]
     for copy in mine:
         copy.start()
@@ -154,7 +156,7 @@
     ext = shape((2, steps + 2 * HALO, 8 * shots), f32)
     built = (
         shape((5, 64, 128), f32), shape((2, 64, 128), f32), shape((2, 256, 576), bf16),
-        shape((16, 256), bf16),
+        shape((80, 256), bf16), shape((16, 256), bf16),
     )
     outs = (ext, ext, shape((spans, 2, 128), f32)) + built
     dma = pltpu.SemaphoreType.DMA
@@ -172,7 +174,7 @@
             pltpu.VMEM((2, 128), f32),
             pltpu.VMEM((2, steps, 128), f32),
         ] + [pltpu.VMEM(a.shape, a.dtype) for a in built] + [pltpu.VMEM(a.shape, a.dtype) for a in staged] + [
-            dma((10,)), dma((6,)), dma((shots,)), dma((shots,)), dma((4,)), dma((4,)), dma((spans,)), dma((spans,)),
+            dma((10,)), dma((7,)), dma((shots,)), dma((shots,)), dma((4,)), dma((4,)), dma((spans,)), dma((spans,)),
         ],
         compiler_params=pltpu.CompilerParams(
             collective_id=0, has_side_effects=True, vmem_limit_bytes=58 * 2**20
@@ -192,15 +194,15 @@
 
 def denoise_kernel(
     spans,
-    dil_in, noisy_in, masked_in, shares_in, cols_in, shot_base_in, wt_in, ow_in, last_in, out,
-    dil, noisy, masked, shares, cols, shot_base, wt, ow, last, sem, x1, x2, state, heads, *sums
+    dil_in, noisy_in, masked_in, shares_in, cols_in, shot_base_in, wt_in, proj_in, last_in, out,
+    dil, noisy, masked, shares, cols, shot_base, wt, proj, last, sem, x1, x2, state, heads, *sums
 ):
     steps = out.shape[1]
     total_time = spans * steps
     sums1, sums2 = sums[:RING], sums[RING:]
     pairs = [
         (dil_in, dil), (noisy_in, noisy), (masked_in, masked), (shares_in, shares), (cols_in, cols),
-        (shot_base_in, shot_base), (wt_in, wt), (ow_in, ow), (last_in, last),
+        (shot_base_in, shot_base), (wt_in, wt), (proj_in, proj), (last_in, last),
     ]
     loads = [pltpu.make_async_copy(a, b, sem.at[i]) for i, (a, b) in enumerate(pairs)]
     for copy in loads:
@@ -211,6 +213,12 @@
     energy = jnp.sum(jnp.sum(shares[...], axis=0), axis=1, keepdims=True)
     scale = lax.rsqrt(jnp.broadcast_to(energy, (2, 128)) / (total_time * 128) + 1e-5)
     first = lax.axis_index("tm") * steps - HALO
+    head_noisy = jnp.sum(cols[4] * cols[0], axis=0, keepdims=True)
+    head_masked = jnp.sum(cols[4] * cols[1], axis=0, keepdims=True)
+    for s in range(2):
+        head_base = jnp.sum(cols[4] * shot_base[s], axis=0, keepdims=True)
+        own = pl.ds(HALO, steps)
+        out[s] = head_noisy * noisy[s, own, :] + head_masked * scale[s : s + 1] * masked[s, own, :] + head_base
     lane = lax.broadcasted_iota(jnp.int32, (64, 128), 1)
     zeros = jnp.zeros((64, 128), bf16)
 
@@ -251,25 +259,29 @@
             lift_row(ahead + q * 8 + u)
         return carry
 
-    before = (2 * d1 + RING + JOINT + 7) // 8
+    before = (2 * d1 + RING + JOINT + 7) // 8 - 1
     lax.fori_loop(0, before, lifts, 0)
     lifted = ahead + before * 8
     for copy in loads[6:]:
         copy.wait()
     for u in range(RING):
         sums1[u][...] = conv(0, x1, start + u, d1)
+    for u in range(8):
+        lift_row(lifted + u)
+    lifted = lifted + 8
 
     def first_end(r, act):
-        updated = state[r] + mm(ow[0], act)
+        delta = mm(proj[...], act)
+        updated = state[r] + delta[:64]
+        heads[r] = delta[64:65, :] + delta[65:66, :]
         halves = [updated[:, s * 128 : (s + 1) * 128] for s in range(2)]
-        heads[r] = jnp.concatenate([jnp.sum(a * cols[4], axis=0, keepdims=True) for a in halves], 1)
         put(x2, r - DMAX, [norm(a, cols[3], r) for a in halves], d2)
 
     def second_end(r, act):
         y = mm(last[...], act)
         y = y[0:1, :] + y[1:2, :] + heads[r + HALO]
         for s in range(2):
-            out[s, pl.ds(r, 1), :] = y[:, s * 128 : (s + 1) * 128]
+            out[s, pl.ds(r, 1), :] += y[:, s * 128 : (s + 1) * 128]
 
     def first_block(r, count):
         for u in range(count):
@@ -334,12 +346,11 @@
         noisy_gather, observed, missing, noise_level, dilations, lift_weight, level_weight,
         norm_gain, conv_weight, out_weight, head_weight,
     ):
-        projections = jnp.swapaxes(out_weight, 1, 2)
-        masked, noisy, shares, cols, shot_base, wt, last = exchange_inputs(
+        masked, noisy, shares, cols, shot_base, wt, proj, last = exchange_inputs(
             shots, spans, jnp.swapaxes(observed, 1, 2), noisy_gather, missing, noise_level[None, :],
-            lift_weight, level_weight[None, :], norm_gain, conv_weight, projections, head_weight[None, :],
-        )
-        return denoise(spans, dilations, noisy, masked, shares, cols, shot_base, wt, projections, last)
+            lift_weight, level_weight[None, :], norm_gain, conv_weight, jnp.swapaxes(out_weight, 1, 2), head_weight[None, :],
+        )
+        return denoise(spans, dilations, noisy, masked, shares, cols, shot_base, wt, proj, last)
 
     return jax.shard_map(
         per_device,

time: 52.2 us -> 49.6 us (0.950)
  Pallas kernels: 52.1 us -> 49.5 us
    pallas_call x1, Pallas kernels: 29.8 us -> 27.2 us  [denoise(): pl.pallas_call(lambda *refs: denoise_kernel(spans, *refs), out_shape=jax....]
where the time goes in v6:
time: 49.6 us; the launch traced here: 49.5 us
  Pallas kernels  49.5 us (100%)
    pallas_call x1, Pallas kernels, denoise(): pl.pallas_call(lambda *refs: denoise_kernel(spans, *refs), out_shape=jax....  27.2 us
    pallas_call x1, Pallas kernels, exchange_inputs(): pl.pallas_call(lambda *refs: exchange_kernel(shots, spans, *refs), out_sh...  22.2 us

profile of v6, /device:TPU:1, one launch (start us, length us, event | category | flops | bytes accessed | tf_op | source)
XLA Modules:
  0.0 49.5 jit_solution(16095228716219955485)
XLA Ops:
  0.0 22.2 %exchange.1 = (f32[2,128,128]{2,1,0:T(8,128)}, f32[2,128,128]{2,1,0:T(8,128)}, f32[16,2,128]{2,1,0:T(2,128)}, f32[5,64,128]{2,1,0:T(8,128)}, f32[2,64,128]{2,1,0...) custom-call(f32[32,8,64]{2,1,0:T(8,128)} %bitcast.5, ...), custom_call_target="tpu_custom_call" | custom-call | tf_op jit(solution)/shard_map/exchange/pallas_call | solution.py:165
  22.2 27.2 %denoise.1 = f32[2,64,128]{2,1,0:T(8,128)} custom-call(s32[2]{0:T(128)} %refs_0_.1, f32[2,128,128]{2,1,0:T(8,128)} %get-tuple-element.13.refs_1_, f32[2,128,128]{2,1,0:T(8,128)} %get-tuple-element.14.refs_2_, f32[16,2,128]{2,1,0:T(2,128)} %get-tuple-element.15.refs_3_, f32[5,64,128]{2,1,0:T(8,128)} %get-tuple-element.16.refs_4_, ...), custom_call_target="tpu_custom_call" | custom-call | tf_op jit(solution)/shard_map/denoise/pallas_call | solution.py:325
